TPU v7x, 512 devices: a whole 4x8x8 slice. The times are simulated.
512 devices in a mesh: table: 128 (over z, y, core), mp: 4 (over x).
Axes of the slice: x: 4, y: 8, z: 8, core: 2. Of those that a mesh axis runs over, the one named last changes fastest.
Arguments:
- replay: bfloat16 [65536, 1024], P('table'), may hold values from -8 to 8
- request_rows: int32 [128, 128, 1], P('table'), may hold values from 0 to 506
- request_count: int32 [128, 128], P('table'), may hold values from 0 to 1
- actions: int32 [5, 16384], P(None, 'table'), may hold values from 0 to 255, as said below
- rewards: float32 [5, 16384], P(None, 'table'), may hold values from -4 to 4
- w_in: bfloat16 [1024, 2048], P('table', 'mp'), may hold values from -0.75 to 0.75
- w_out: bfloat16 [1024, 2048], P('table', 'mp'), may hold values from -1 to 1
- w_pol: bfloat16 [1024, 256], replicated, may hold values from -4 to 4
- w_val: bfloat16 [1024], replicated, may hold values from -0.1875 to 0.1875
- embed: bfloat16 [256, 1024], replicated, may hold values from -6 to 6
- gain: float32 [1024], replicated, may hold values from 0.5 to 1.5
Outputs:
- grad_pol: float32 [1024, 256], P('table')
- grad_embed: float32 [256, 1024], P('table')
- grad_val: float32 [1024], P('table')
Inputs may be any that keep to these rules, and one draw needn't show every extreme that they name: `request_rows`: each names the first of 6 consecutive rows of the owner's shard. `request_count`: slots below the count are used, the others are padding. The law of an unroll's actions depends on its requester and its owner.
All inputs are finite; a program needn't handle non-finite values.
Results may differ from a plain program's by a relative error of at most 0.025.
Values may be sent and summed in bfloat16 or wider, within the bound.
No kernel may reach another device: no remote copies, remote signals or barrier semaphores. Data moves between devices by JAX's collectives and lax.ppermute only.
A program may use at most 64 MiB of HBM per device.

v0:
```python
import jax
import jax.numpy as jnp
from jax import lax
from jax.sharding import PartitionSpec as P

discount = 0.997
epsilon = 1e-06


def normalize(vector, gain):
    factor = lax.rsqrt(jnp.mean(vector * vector, axis=-1, keepdims=True) + epsilon)
    return vector * factor * gain


def norm_back(vector, upstream, gain):
    factor = lax.rsqrt(jnp.mean(vector * vector, axis=-1, keepdims=True) + epsilon)
    unit_vec = vector * factor
    scaled = upstream * gain
    return factor * (scaled - unit_vec * jnp.mean(scaled * unit_vec, axis=-1, keepdims=True))


def cols_product(left, weight):
    return lax.dot_general(
        left, weight, (((1,), (1,)), ((), ())), preferred_element_type=jnp.float32
    )


def per_device(
    replay, request_rows, request_count, actions, rewards, w_in, w_out, w_pol, w_val, embed, gain
):
    table_count = lax.axis_size("table")
    features = replay.shape[1]
    unroll_len = actions.shape[0]
    slot_count = request_rows.shape[2]
    num_actions = w_pol.shape[1]
    group_size = table_count * slot_count
    offsets = jnp.arange(unroll_len + 1, dtype=jnp.int32)
    positions_all = request_rows[0][None, :, :] + offsets[:, None, None]
    used_flags = (
        jnp.arange(slot_count, dtype=jnp.int32)[None, :] < request_count[0][:, None]
    ).astype(jnp.bfloat16)[None]
    picked = jnp.take(replay, positions_all, axis=0)
    arrived, flags = (
        lax.all_to_all(picked, "table", split_axis=1, concat_axis=1, tiled=True),
        lax.all_to_all(used_flags, "table", split_axis=1, concat_axis=1, tiled=True),
    )
    observed = arrived.reshape(unroll_len + 1, group_size, features)
    used_rows = flags.reshape(group_size).astype(jnp.float32)
    full_in, full_out = (
        lax.all_gather(w_in, "table", axis=0, tiled=True),
        lax.all_gather(w_out, "table", axis=0, tiled=True),
    )
    own_rows = observed.shape[1]
    flat_obs = observed.reshape((unroll_len + 1) * own_rows, features).astype(jnp.float32)
    target_in = normalize(flat_obs, gain).astype(jnp.bfloat16)
    target_logits = jnp.dot(target_in, w_pol, preferred_element_type=jnp.float32)
    target_values = jnp.dot(target_in, w_val, preferred_element_type=jnp.float32).reshape(
        unroll_len + 1, own_rows
    )
    policy_targets = jax.nn.softmax(target_logits, axis=-1)
    value_targets = jnp.concatenate(
        [rewards + discount * target_values[1:], target_values[unroll_len:]], axis=0
    )
    action_ids = jnp.arange(num_actions, dtype=jnp.int32)
    latent = observed[0].astype(jnp.float32)
    latents = [latent]
    mixeds = []
    preacts = []
    onehots = []
    for position in range(unroll_len):
        onehot = (actions[position][:, None] == action_ids[None, :]).astype(jnp.bfloat16)
        mixed = latent + jnp.dot(onehot, embed, preferred_element_type=jnp.float32)
        normed = normalize(mixed, gain).astype(jnp.bfloat16)
        preact = jnp.dot(normed, full_in, preferred_element_type=jnp.float32)
        hidden = jax.nn.silu(preact).astype(jnp.bfloat16)
        latent = mixed + lax.psum(cols_product(hidden, full_out).astype(jnp.bfloat16), "mp").astype(
            jnp.float32
        )
        latents.append(latent)
        mixeds.append(mixed)
        preacts.append(preact)
        onehots.append(onehot)
    stacked = jnp.stack(latents).reshape((unroll_len + 1) * own_rows, features)
    head_in = normalize(stacked, gain).astype(jnp.bfloat16)
    logits = jnp.dot(head_in, w_pol, preferred_element_type=jnp.float32)
    values = jnp.dot(head_in, w_val, preferred_element_type=jnp.float32)
    row_weight = jnp.tile(used_rows / group_size, unroll_len + 1)
    logit_grad = (row_weight[:, None] * (jax.nn.softmax(logits, axis=-1) - policy_targets)).astype(
        jnp.bfloat16
    )
    value_grad = 2.0 * row_weight * (values - value_targets.reshape(-1))
    grad_pol = lax.dot_general(
        head_in, logit_grad, (((0,), (0,)), ((), ())), preferred_element_type=jnp.float32
    )
    grad_val = jnp.sum(head_in.astype(jnp.float32) * value_grad[:, None], axis=0)
    head_grad = (
        jnp.dot(logit_grad, w_pol.T, preferred_element_type=jnp.float32)
        + value_grad[:, None] * w_val.astype(jnp.float32)[None, :]
    )
    head_back = norm_back(stacked, head_grad, gain).reshape(unroll_len + 1, own_rows, features)
    cotangent = head_back[unroll_len]
    grad_embed = jnp.zeros((num_actions, features), jnp.float32)
    for position in reversed(range(unroll_len)):
        hidden_grad = jnp.dot(
            cotangent.astype(jnp.bfloat16), full_out, preferred_element_type=jnp.float32
        )
        sigmoid_val = jax.nn.sigmoid(preacts[position])
        preact_grad = (
            hidden_grad * sigmoid_val * (1.0 + preacts[position] * (1.0 - sigmoid_val))
        ).astype(jnp.bfloat16)
        normed_grad = lax.psum(
            cols_product(preact_grad, full_in).astype(jnp.bfloat16), "mp"
        ).astype(jnp.float32)
        mixed_grad = cotangent + norm_back(mixeds[position], normed_grad, gain)
        grad_embed = grad_embed + lax.dot_general(
            onehots[position],
            mixed_grad.astype(jnp.bfloat16),
            (((0,), (0,)), ((), ())),
            preferred_element_type=jnp.float32,
        )
        cotangent = mixed_grad + head_back[position]
    out_pol, out_embed, out_val = (
        lax.psum_scatter(grad_pol, "table", scatter_dimension=0, tiled=True),
        lax.psum_scatter(grad_embed, "table", scatter_dimension=0, tiled=True),
        lax.psum_scatter(grad_val, "table", scatter_dimension=0, tiled=True),
    )
    return (out_pol, out_embed, out_val)


def solution(mesh):
    return jax.shard_map(
        per_device,
        mesh=mesh,
        in_specs=(
            P("table", None),
            P("table", None, None),
            P("table", None),
            P(None, "table"),
            P(None, "table"),
            P("table", "mp"),
            P("table", "mp"),
            P(),
            P(),
            P(),
            P(),
        ),
        out_specs=(P("table", None), P("table", None), P("table")),
        check_vma=False,
    )
```

profile of v0, /device:TPU:2, one launch (start us, length us, event | category | flops | bytes accessed | tf_op | source)
XLA Modules:
  0.0 1212.3 jit_solution(7820904012027257947)
XLA Ops:
  13.9 18.5 %all-to-all-start = ((bf16[6,128,1,1024]{3,0,2,1:T(8,128)(2,1)}), bf16[6,128,1,1024]{3,0,2,1:T(8,128)(2,1)}, u32[]{:S(2)}, u32[]{:S(2)}) async-start(bf16[6,128,1,1024]{3,0,2,1:T(8,128)(2,1)} %copy_select_fusion), calls=%async_computation | async-start | bytes 4194304 | tf_op jit(solution)/shard_map/all_to_all | solution.py:44
  34.0 50.6 %all-to-all-done = bf16[6,128,1,1024]{3,0,2,1:T(8,128)(2,1)} async-done(((bf16[6,128,1,1024]{3,0,2,1:T(8,128)(2,1)}), bf16[6,128,1,1024]{3,0,2,1:T(8,128)(2,1)}, u32[]{:S(2)}, u32[]{:S(2)}) %all-to-all-start) | async-done | bytes 1572896 | tf_op jit(solution)/shard_map/all_to_all | solution.py:44
  88.6 48.5 %all-gather.3.cloned.1.call-done = bf16[1024,512]{1,0:T(8,128)(2,1)} async-done(((bf16[8,512]{1,0:T(8,128)(2,1)}), bf16[1024,512]{1,0:T(8,128)(2,1)}) %all-gather.3.cloned.1.call-update) | async-done | bytes 1048592 | tf_op jit(solution)/shard_map/all_gather | solution.py:50
  138.8 76.3 %all-gather.5.cloned.1.call-done = bf16[1024,512]{1,0:T(8,128)(2,1)} async-done(((bf16[8,512]{1,0:T(8,128)(2,1)}), bf16[1024,512]{1,0:T(8,128)(2,1)}) %all-gather.5.cloned.1.call-update) | async-done | bytes 1048592 | tf_op jit(solution)/shard_map/all_gather | solution.py:51
  218.3 8.8 all-to-all-start.1
  227.3 37.6 %all-reduce.14.cloned.1.call-done = bf16[128,1024]{1,0:T(8,128)(2,1)} async-done(((bf16[128,1024]{1,0:T(8,128)(2,1)}), bf16[128,1024]{1,0:T(8,128)(2,1)}) %all-reduce.14.cloned.1.call-update) | async-done | bytes 262160 | tf_op jit(solution)/shard_map/psum | solution.py:76
  270.4 51.4 %all-reduce.16.cloned.1.call-done = bf16[128,1024]{1,0:T(8,128)(2,1)} async-done(((bf16[128,1024]{1,0:T(8,128)(2,1)}), bf16[128,1024]{1,0:T(8,128)(2,1)}) %all-reduce.16.cloned.1.call-update) | async-done | bytes 262160 | tf_op jit(solution)/shard_map/psum | solution.py:76
  328.2 51.2 %all-reduce.18.cloned.1.call-done = bf16[128,1024]{1,0:T(8,128)(2,1)} async-done(((bf16[128,1024]{1,0:T(8,128)(2,1)}), bf16[128,1024]{1,0:T(8,128)(2,1)}) %all-reduce.18.cloned.1.call-update) | async-done | bytes 262160 | tf_op jit(solution)/shard_map/psum | solution.py:76
  387.2 50.1 %all-reduce.20.cloned.1.call-done = bf16[128,1024]{1,0:T(8,128)(2,1)} async-done(((bf16[128,1024]{1,0:T(8,128)(2,1)}), bf16[128,1024]{1,0:T(8,128)(2,1)}) %all-reduce.20.cloned.1.call-update) | async-done | bytes 262160 | tf_op jit(solution)/shard_map/psum | solution.py:76
  446.2 49.1 %all-reduce.22.cloned.1.call-done = bf16[128,1024]{1,0:T(8,128)(2,1)} async-done(((bf16[128,1024]{1,0:T(8,128)(2,1)}), bf16[128,1024]{1,0:T(8,128)(2,1)}) %all-reduce.22.cloned.1.call-update) | async-done | bytes 262160 | tf_op jit(solution)/shard_map/psum | solution.py:76
  509.1 2.9 convolution_convert_fusion.4
  512.1 53.0 %all-reduce.24.cloned.1.call-done = bf16[128,1024]{1,0:T(8,128)(2,1)} async-done(((bf16[128,1024]{1,0:T(8,128)(2,1)}), bf16[128,1024]{1,0:T(8,128)(2,1)}) %all-reduce.24.cloned.1.call-update) | async-done | bytes 262160 | tf_op jit(solution)/shard_map/psum | solution.py:111
  568.7 3.0 convolution_convert_fusion.3
  574.3 50.5 %all-reduce.26.cloned.1.call-done = bf16[128,1024]{1,0:T(8,128)(2,1)} async-done(((bf16[128,1024]{1,0:T(8,128)(2,1)}), bf16[128,1024]{1,0:T(8,128)(2,1)}) %all-reduce.26.cloned.1.call-update) | async-done | bytes 262160 | tf_op jit(solution)/shard_map/psum | solution.py:111
  628.5 3.0 convolution_convert_fusion.2
  631.6 2.8 convolution_add_fusion.3
  634.4 50.2 %all-reduce.28.cloned.1.call-done = bf16[128,1024]{1,0:T(8,128)(2,1)} async-done(((bf16[128,1024]{1,0:T(8,128)(2,1)}), bf16[128,1024]{1,0:T(8,128)(2,1)}) %all-reduce.28.cloned.1.call-update) | async-done | bytes 262160 | tf_op jit(solution)/shard_map/psum | solution.py:111
  688.4 3.0 convolution_convert_fusion.1
  694.3 50.2 %all-reduce.30.cloned.1.call-done = bf16[128,1024]{1,0:T(8,128)(2,1)} async-done(((bf16[128,1024]{1,0:T(8,128)(2,1)}), bf16[128,1024]{1,0:T(8,128)(2,1)}) %all-reduce.30.cloned.1.call-update) | async-done | bytes 262160 | tf_op jit(solution)/shard_map/psum | solution.py:111
  747.9 3.1 convolution_convert_fusion
  752.7 51.3 %all-reduce.32.cloned.1.call-done = bf16[128,1024]{1,0:T(8,128)(2,1)} async-done(((bf16[128,1024]{1,0:T(8,128)(2,1)}), bf16[128,1024]{1,0:T(8,128)(2,1)}) %all-reduce.32.cloned.1.call-update) | async-done | bytes 262160 | tf_op jit(solution)/shard_map/psum | solution.py:111
  807.9 3.1 fusion.101
  815.9 250.5 %all-reduce.1 = f32[1024]{0:T(1024)S(1)} all-reduce(f32[1024]{0:T(1024)S(1)} %multiply_reduce_fusion), channel_id=4, replica_groups=mesh['table'=128,'mp'=4] {'table'}, use_global_device_ids=true, to_apply=%region_30.31.clone | all-reduce | flops 1024 | bytes 8192
  1068.4 137.4 %reduce-scatter.2.cloned.1.call-done = f32[8,256]{1,0:T(8,128)} async-done(((f32[1024,256]{1,0:T(8,128)}), f32[8,256]{1,0:T(8,128)}) %reduce-scatter.2.cloned.1.call-update) | async-done | bytes 8208 | tf_op jit(solution)/shard_map/reduce_scatter | solution.py:123
  (192 shorter events, 90.5 us)
Async XLA Ops:
  13.9 70.7 %all-to-all-start = ((bf16[6,128,1,1024]{3,0,2,1:T(8,128)(2,1)}), bf16[6,128,1,1024]{3,0,2,1:T(8,128)(2,1)}, u32[]{:S(2)}, u32[]{:S(2)}) async-start(bf16[6,128,1,1024]{3,0,2,1:T(8,128)(2,1)} %copy_select_fusion), calls=%async_computation | async-start | bytes 4194304 | tf_op jit(solution)/shard_map/all_to_all | solution.py:44
  32.4 104.7 %all-gather.3.cloned.1.call-start = ((), (), s32[]{:S(2)}) async-start(), calls=%async_computation.3 | async-start | bytes 1056768 | tf_op jit(solution)/shard_map/all_gather | solution.py:50
  33.2 181.9 %all-gather.5.cloned.1.call-start = ((), (), s32[]{:S(2)}) async-start(), calls=%async_computation.4 | async-start | bytes 1056768 | tf_op jit(solution)/shard_map/all_gather | solution.py:51
  33.9 230.9 %all-reduce.14.cloned.1.call-start = ((), (), s32[]{:S(2)}) async-start(), calls=%async_computation.5 | async-start | bytes 524288 | tf_op jit(solution)/shard_map/psum | solution.py:76
  34.0 230.8 %copy-start.33 = (s32[128]{0:T(128)}, s32[128]{0:T(128)S(1)}, u32[]{:S(2)}) copy-start(s32[128]{0:T(128)S(1)} %get-tuple-element.11) | copy-start | bytes 1540
  34.0 287.8 %copy-start.35 = (s32[128]{0:T(128)}, s32[128]{0:T(128)S(1)}, u32[]{:S(2)}) copy-start(s32[128]{0:T(128)S(1)} %get-tuple-element.10) | copy-start | bytes 1540
  34.0 345.4 %copy-start.36 = (s32[128]{0:T(128)}, s32[128]{0:T(128)S(1)}, u32[]{:S(2)}) copy-start(s32[128]{0:T(128)S(1)} %get-tuple-element.13) | copy-start | bytes 1540
  34.0 403.3 %copy-start.25 = (s32[128]{0:T(128)}, s32[128]{0:T(128)S(1)}, u32[]{:S(2)}) copy-start(s32[128]{0:T(128)S(1)} %get-tuple-element.9) | copy-start | bytes 1540
  87.5 130.1 %copy-start.41 = (s32[1,128]{1,0:T(1,128)S(1)}, s32[1,128]{1,0:T(1,128)}, u32[]{:S(2)}) copy-start(s32[1,128]{1,0:T(1,128)} %param.13) | copy-start | bytes 1540
  87.5 139.8 %copy-start.24 = (bf16[1024]{0:T(1024)(128)(2,1)S(1)}, bf16[1024]{0:T(1024)(128)(2,1)}, u32[]{:S(2)}) copy-start(bf16[1024]{0:T(1024)(128)(2,1)} %param.19) | copy-start | bytes 6148
  88.6 178.2 %copy-start.38 = (f32[128]{0:T(128)}, f32[128]{0:T(128)S(1)}, u32[]{:S(2)}) copy-start(f32[128]{0:T(128)S(1)} %add_rsqrt_fusion.5) | copy-start | bytes 1540
  138.8 129.9 %copy-start.16 = (f32[128,512]{1,0:T(8,128)}, f32[128,512]{1,0:T(8,128)S(1)}, u32[]{:S(2)}) copy-start(f32[128,512]{1,0:T(8,128)S(1)} %fusion.15) | copy-start | bytes 786436
  218.3 50.4 %all-to-all-start.1 = ((bf16[1,128,1]{2,0,1:T(2,128)(2,1)}), bf16[1,128,1]{2,0,1:T(2,128)(2,1)S(1)}, u32[]{:S(2)}, u32[]{:S(2)}) async-start(bf16[1,128,1]{2,0,1:T(2,128)(2,1)} %copy.45), calls=%async_computation.1 | async-start | bytes 131072 | tf_op jit(solution)/shard_map/all_to_all | solution.py:45
  227.2 94.6 %all-reduce.16.cloned.1.call-start = ((), (), s32[]{:S(2)}) async-start(), calls=%async_computation.6 | async-start | bytes 524288 | tf_op jit(solution)/shard_map/psum | solution.py:76
  268.7 110.7 %all-reduce.18.cloned.1.call-start = ((), (), s32[]{:S(2)}) async-start(), calls=%async_computation.7 | async-start | bytes 524288 | tf_op jit(solution)/shard_map/psum | solution.py:76
  326.4 111.0 %all-reduce.20.cloned.1.call-start = ((), (), s32[]{:S(2)}) async-start(), calls=%async_computation.8 | async-start | bytes 524288 | tf_op jit(solution)/shard_map/psum | solution.py:76
  384.3 111.0 %all-reduce.22.cloned.1.call-start = ((), (), s32[]{:S(2)}) async-start(), calls=%async_computation.9 | async-start | bytes 524288 | tf_op jit(solution)/shard_map/psum | solution.py:76
  442.2 122.9 %all-reduce.24.cloned.1.call-start = ((), (), s32[]{:S(2)}) async-start(), calls=%async_computation.11 | async-start | bytes 524288 | tf_op jit(solution)/shard_map/psum | solution.py:111
  512.0 112.7 %all-reduce.26.cloned.1.call-start = ((), (), s32[]{:S(2)}) async-start(), calls=%async_computation.12 | async-start | bytes 524288 | tf_op jit(solution)/shard_map/psum | solution.py:111
  571.7 112.9 %all-reduce.28.cloned.1.call-start = ((), (), s32[]{:S(2)}) async-start(), calls=%async_computation.13 | async-start | bytes 524288 | tf_op jit(solution)/shard_map/psum | solution.py:111
  631.5 112.9 %all-reduce.30.cloned.1.call-start = ((), (), s32[]{:S(2)}) async-start(), calls=%async_computation.14 | async-start | bytes 524288 | tf_op jit(solution)/shard_map/psum | solution.py:111
  691.4 112.6 %all-reduce.32.cloned.1.call-start = ((), (), s32[]{:S(2)}) async-start(), calls=%async_computation.15 | async-start | bytes 524288 | tf_op jit(solution)/shard_map/psum | solution.py:111
  751.0 316.0 %all-reduce.34.cloned.1.call-start = ((), (), s32[]{:S(2)}) async-start(), calls=%async_computation.16 | async-start | bytes 2097152
  807.9 398.0 %reduce-scatter.2.cloned.1.call-start = ((), (), s32[]{:S(2)}) async-start(), calls=%async_computation.10 | async-start | bytes 1056768 | tf_op jit(solution)/shard_map/reduce_scatter | solution.py:123
  (34 other events, 830.4 us)
Sparse Core Ops, SparseCore 0:
  36.3 100.8 all-gather.2
  140.2 74.8 all-gather.4
  217.7 47.1 all-reduce.13
  268.8 52.8 all-reduce.15
  326.5 52.8 all-reduce.17
  384.4 52.8 all-reduce.19
  442.4 52.8 all-reduce.21
  512.2 52.8 all-reduce.23
  571.8 52.8 all-reduce.25
  631.7 52.8 all-reduce.27
  691.5 52.8 all-reduce.29
  751.1 52.8 all-reduce.31
  808.0 197.6 all-reduce.33
  1010.4 195.3 reduce-scatter.1
where the time goes:
time: 1210 us
  waiting for transfers between devices  809 us (67%)
  blocking collectives  250 us (21%)
  matrix products  51.3 us (4%)
  other arithmetic  43.6 us (4%)
  starting transfers between devices  28.1 us (2%)
  between operations  15.9 us (1%)
  local copies, waits for them, and re-layouts  14.2 us (1%)
    psum x5, waiting for transfers between devices, per_device(): lax.psum(cols_product(preact_grad, full_in).astype(jnp.bfloat16), 'mp')  255 us
    unnamed x1, blocking collectives  250 us
    psum x5, waiting for transfers between devices, per_device(): lax.psum(cols_product(hidden, full_out).astype(jnp.bfloat16), 'mp')  239 us
    reduce_scatter x1, waiting for transfers between devices, per_device(): lax.psum_scatter(grad_pol, 'table', scatter_dimension=0, tiled=True)  137 us
    all_gather x1, waiting for transfers between devices, per_device(): lax.all_gather(w_out, 'table', axis=0, tiled=True)  76.3 us
    all_to_all x1, waiting for transfers between devices, per_device(): lax.all_to_all(picked, 'table', split_axis=1, concat_axis=1, tiled=True)  50.6 us
    all_gather x1, waiting for transfers between devices, per_device(): lax.all_gather(w_in, 'table', axis=0, tiled=True)  48.5 us
  transfers between devices with their start and end apart: 16, of which 14 were waited for; matrix products, arithmetic and copies ran while one was open for 3% of the time, Pallas kernels for 0%

commit v1 on v0

v1 whole, which is shorter than its diff:
```python
import jax
import jax.numpy as jnp
from jax import lax
from jax.sharding import PartitionSpec as P

discount = 0.997
epsilon = 1e-06


def normalize(vector, gain):
    factor = lax.rsqrt(jnp.mean(vector * vector, axis=-1, keepdims=True) + epsilon)
    return vector * factor * gain


def norm_back(vector, upstream, gain):
    factor = lax.rsqrt(jnp.mean(vector * vector, axis=-1, keepdims=True) + epsilon)
    unit_vec = vector * factor
    scaled = upstream * gain
    return factor * (scaled - unit_vec * jnp.mean(scaled * unit_vec, axis=-1, keepdims=True))


def cols_product(left, weight):
    return lax.dot_general(
        left, weight, (((1,), (1,)), ((), ())), preferred_element_type=jnp.float32
    )


def rows_product(left, right):
    return lax.dot_general(
        left, right, (((0,), (0,)), ((), ())), preferred_element_type=jnp.float32
    )


def fetch_unrolls(replay, request_rows, request_count, steps, tables, members):
    member = lax.axis_index("mp")
    share = tables // members
    width = replay.shape[1]
    firsts = request_rows[0, :, 0].reshape(share, members)
    firsts = lax.dynamic_index_in_dim(firsts, member, 1, keepdims=False)
    counts = lax.dynamic_index_in_dim(
        request_count[0].reshape(share, members), member, 1, keepdims=False
    )
    used = (counts > 0).astype(jnp.float32)
    offsets = jnp.arange(8, dtype=jnp.int32)
    positions = firsts[:, None] + offsets[None, :]
    row_ids = jnp.arange(replay.shape[0], dtype=jnp.int32)
    picks = (positions.reshape(-1)[:, None] == row_ids[None, :]).astype(jnp.bfloat16)
    rows = jnp.dot(picks, replay, preferred_element_type=jnp.float32).reshape(share, 8, width)
    rows = jnp.where(offsets[None, :, None] <= steps, rows, used[:, None, None])
    rows = rows.astype(jnp.bfloat16)
    swap = [
        ((members * a + b) * members + d, (members * a + d) * members + b)
        for a in range(share)
        for b in range(members)
        for d in range(members)
    ]
    rows = lax.ppermute(rows, ("table", "mp"), swap)
    groups = [[members * a + d for a in range(share)] for d in range(members)]
    rows = lax.all_to_all(
        rows, "table", split_axis=0, concat_axis=0, tiled=True, axis_index_groups=groups
    )
    observed = rows[:, : steps + 1].transpose(1, 0, 2)
    return observed, rows[:, steps + 1, 0].astype(jnp.float32)


def gather_weights(w_in, w_out, tables, members):
    both = jnp.concatenate([w_in, w_out], axis=0)
    full = lax.all_gather(both, ("table", "mp"), axis=0, tiled=True)
    rows, cols = w_in.shape
    full = full.reshape(tables, members, 2, rows, cols).transpose(2, 0, 3, 1, 4)
    full = full.reshape(2, tables * rows, members * cols)
    return full[0], full[1]


def sum_over_tables(partial, tables):
    sent = partial.astype(jnp.bfloat16)
    parts = lax.all_to_all(sent, "table", split_axis=0, concat_axis=0, tiled=True)
    return jnp.sum(parts.astype(jnp.float32), axis=0)


def per_device(
    replay, request_rows, request_count, actions, rewards, w_in, w_out, w_pol, w_val, embed, gain
):
    tables = lax.axis_size("table")
    members = lax.axis_size("mp")
    member = lax.axis_index("mp")
    share = tables // members
    features = replay.shape[1]
    steps = actions.shape[0]
    num_actions = w_pol.shape[1]
    full_in, full_out = gather_weights(w_in, w_out, tables, members)
    observed, used_rows = fetch_unrolls(
        replay, request_rows, request_count, steps, tables, members
    )
    actions = lax.dynamic_index_in_dim(
        actions.reshape(steps, share, members), member, 2, keepdims=False
    )
    rewards = lax.dynamic_index_in_dim(
        rewards.reshape(steps, share, members), member, 2, keepdims=False
    )
    flat_obs = observed.reshape((steps + 1) * share, features).astype(jnp.float32)
    target_in = normalize(flat_obs, gain).astype(jnp.bfloat16)
    target_logits = jnp.dot(target_in, w_pol, preferred_element_type=jnp.float32)
    target_values = jnp.dot(target_in, w_val, preferred_element_type=jnp.float32).reshape(
        steps + 1, share
    )
    policy_targets = jax.nn.softmax(target_logits, axis=-1)
    value_targets = jnp.concatenate(
        [rewards + discount * target_values[1:], target_values[steps:]], axis=0
    )
    action_ids = jnp.arange(num_actions, dtype=jnp.int32)
    latent = observed[0].astype(jnp.float32)
    latents = [latent]
    mixeds = []
    preacts = []
    onehots = []
    for position in range(steps):
        onehot = (actions[position][:, None] == action_ids[None, :]).astype(jnp.bfloat16)
        mixed = latent + jnp.dot(onehot, embed, preferred_element_type=jnp.float32)
        normed = normalize(mixed, gain).astype(jnp.bfloat16)
        preact = jnp.dot(normed, full_in, preferred_element_type=jnp.float32)
        hidden = jax.nn.silu(preact).astype(jnp.bfloat16)
        latent = mixed + cols_product(hidden, full_out)
        latents.append(latent)
        mixeds.append(mixed)
        preacts.append(preact)
        onehots.append(onehot)
    stacked = jnp.stack(latents).reshape((steps + 1) * share, features)
    head_in = normalize(stacked, gain).astype(jnp.bfloat16)
    logits = jnp.dot(head_in, w_pol, preferred_element_type=jnp.float32)
    values = jnp.dot(head_in, w_val, preferred_element_type=jnp.float32)
    row_weight = jnp.tile(used_rows / tables, steps + 1)
    logit_grad = (row_weight[:, None] * (jax.nn.softmax(logits, axis=-1) - policy_targets)).astype(
        jnp.bfloat16
    )
    value_grad = 2.0 * row_weight * (values - value_targets.reshape(-1))
    grad_pol = rows_product(head_in, logit_grad)
    grad_val = jnp.sum(head_in.astype(jnp.float32) * value_grad[:, None], axis=0)
    head_grad = (
        cols_product(logit_grad, w_pol)
        + value_grad[:, None] * w_val.astype(jnp.float32)[None, :]
    )
    rows_pol = features // tables
    lane = jnp.arange(128, dtype=jnp.int32)
    val_block = jnp.where(lane == 0, grad_val.reshape(tables, rows_pol, 1), 0.0)
    pol_val = jnp.concatenate([grad_pol.reshape(tables, rows_pol, num_actions), val_block], axis=2)
    pol_val = sum_over_tables(pol_val, tables)
    head_back = norm_back(stacked, head_grad, gain).reshape(steps + 1, share, features)
    cotangent = head_back[steps]
    mixed_lows = []
    for position in reversed(range(steps)):
        hidden_grad = jnp.dot(
            cotangent.astype(jnp.bfloat16), full_out, preferred_element_type=jnp.float32
        )
        sigmoid_val = jax.nn.sigmoid(preacts[position])
        preact_grad = (
            hidden_grad * sigmoid_val * (1.0 + preacts[position] * (1.0 - sigmoid_val))
        ).astype(jnp.bfloat16)
        normed_grad = cols_product(preact_grad, full_in)
        mixed_grad = cotangent + norm_back(mixeds[position], normed_grad, gain)
        mixed_lows.append(mixed_grad.astype(jnp.bfloat16))
        cotangent = mixed_grad + head_back[position]
    grad_embed = rows_product(
        jnp.concatenate(onehots[::-1], axis=0), jnp.concatenate(mixed_lows, axis=0)
    )
    rows_embed = num_actions // tables
    embed_sum = sum_over_tables(grad_embed.reshape(tables, rows_embed * features // 128, 128), tables)
    packed = jnp.concatenate([pol_val.reshape(-1, 128), embed_sum], axis=0)
    lines = [[t * members + m for m in range(members)] for t in range(tables)]
    packed = lax.psum(packed, ("table", "mp"), axis_index_groups=lines)
    cut = pol_val.size // 128
    pol_val = packed[:cut].reshape(rows_pol, num_actions + 128)
    out_embed = packed[cut:].reshape(rows_embed, features)
    return pol_val[:, :num_actions], out_embed, pol_val[:, num_actions]


def solution(mesh):
    return jax.shard_map(
        per_device,
        mesh=mesh,
        in_specs=(
            P("table", None),
            P("table", None, None),
            P("table", None),
            P(None, "table"),
            P(None, "table"),
            P("table", "mp"),
            P("table", "mp"),
            P(),
            P(),
            P(),
            P(),
        ),
        out_specs=(P("table", None), P("table", None), P("table")),
        check_vma=False,
    )
```

time: 1210 us -> 313 us (0.26)
  the two profiles are of different devices: /device:TPU:2 before, /device:TPU:8 now
where the time goes in v1:
time: 313 us; the launch traced here: 312 us
  waiting for transfers between devices  155 us (50%)
  matrix products  55.7 us (18%)
  starting transfers between devices  36 us (12%)
  other arithmetic  21 us (7%)
  local copies, waits for them, and re-layouts  14.8 us (5%)
  blocking collectives  14.8 us (5%)
  between operations  14.8 us (5%)
    all_gather x1, waiting for transfers between devices, gather_weights(): full = lax.all_gather(both, ('table', 'mp'), axis=0, tiled=True)  87.9 us
    dot_general x11, matrix products, cols_product(): lax.dot_general(left, weight, (((1,), (1,)), ((), ())), preferred_element...  41.8 us
    all_to_all x2, waiting for transfers between devices, sum_over_tables(): lax.all_to_all(sent, 'table', split_axis=0, concat_axis=0, tiled=True)  41.3 us
    all_to_all x1, waiting for transfers between devices, fetch_unrolls(): lax.all_to_all(rows, 'table', split_axis=0, concat_axis=0, tiled=True, ax...  16.1 us
    all_to_all x2, starting transfers between devices, sum_over_tables(): lax.all_to_all(sent, 'table', split_axis=0, concat_axis=0, tiled=True)  16 us
    all_to_all x1, starting transfers between devices, fetch_unrolls(): lax.all_to_all(rows, 'table', split_axis=0, concat_axis=0, tiled=True, ax...  15.1 us
    psum x1, blocking collectives, per_device(): packed = lax.psum(packed, ('table', 'mp'), axis_index_groups=lines)  14.8 us
    ppermute x1, waiting for transfers between devices, fetch_unrolls(): rows = lax.ppermute(rows, ('table', 'mp'), swap)  9.86 us
  transfers between devices with their start and end apart: 5, of which 5 were waited for; matrix products, arithmetic and copies ran while one was open for 5% of the time, Pallas kernels for 0%

profile of v1, /device:TPU:8, one launch (start us, length us, event | category | flops | bytes accessed | tf_op | source)
XLA Modules:
  0.0 312.4 jit_solution(4806825717596081949)
XLA Ops:
  13.1 4.8 %collective-permute-start = (bf16[32,8,1024]{2,1,0:T(8,128)(2,1)S(1)}, bf16[32,8,1024]{2,1,0:T(8,128)(2,1)}, u32[]{:S(2)}, u32[]{:S(2)}) collective-permute-start(bf16[32,8,1024]{2,1,0:T(8,128)(2,1)S(1)} %fusion.11), channel_id=1, source_target_pairs={{0,0},{1,4},{2,8},{3,12},{4,1},{5,5},{6,9},{7,13},{8,2},{9,6},{10,... | collective-permute-start | bytes 1572872 | tf_op jit(solution)/shard_map/ppermute | solution.py:57
  21.9 9.9 %collective-permute-done = bf16[32,8,1024]{2,1,0:T(8,128)(2,1)} collective-permute-done((bf16[32,8,1024]{2,1,0:T(8,128)(2,1)S(1)}, bf16[32,8,1024]{2,1,0:T(8,128)(2,1)}, u32[]{:S(2)}, u32[]{:S(2)}) %collective-permute-start) | collective-permute-done | bytes 524320 | tf_op jit(solution)/shard_map/ppermute | solution.py:57
  31.8 15.1 %all-to-all-start = ((bf16[32,8,1024]{2,1,0:T(8,128)(2,1)}), bf16[32,8,1024]{2,1,0:T(8,128)(2,1)S(1)}, u32[]{:S(2)}, u32[]{:S(2)}) async-start(bf16[32,8,1024]{2,1,0:T(8,128)(2,1)} %collective-permute-done), calls=%async_computation | async-start | bytes 1048576 | tf_op jit(solution)/shard_map/all_to_all | solution.py:59
  47.3 16.1 %all-to-all-done = bf16[32,8,1024]{2,1,0:T(8,128)(2,1)S(1)} async-done(((bf16[32,8,1024]{2,1,0:T(8,128)(2,1)}), bf16[32,8,1024]{2,1,0:T(8,128)(2,1)S(1)}, u32[]{:S(2)}, u32[]{:S(2)}) %all-to-all-start) | async-done | bytes 524320 | tf_op jit(solution)/shard_map/all_to_all | solution.py:59
  65.8 87.9 %all-gather.2.cloned.1.call-done = bf16[8192,512]{1,0:T(8,128)(2,1)} async-done(((bf16[16,512]{1,0:T(8,128)(2,1)}), bf16[8192,512]{1,0:T(8,128)(2,1)}) %all-gather.2.cloned.1.call-update) | async-done | bytes 8388624 | tf_op jit(solution)/shard_map/all_gather | solution.py:68
  153.8 4.0 %fusion.98 = (bf16[1,128,8,4,512]{4,2,0,3,1:T(8,128)(2,1)S(1)}, bf16[1,128,8,4,512]{4,2,0,3,1:T(8,128)(2,1)S(1)}) fusion(bf16[2,128,8,4,512]{4,2,0,3,1:T(8,128)(2,1)} %bitcast.107), kind=kLoop, calls=%fused_computation.219 | loop fusion | bytes 16777216 | tf_op jit(solution)/shard_map/slice | solution.py:72
  172.5 2.0 fusion.99
  174.7 2.0 fusion.100
  178.2 1.7 multiply_reduce_fusion
  181.4 7.0 %multiply_reduce_fusion.8 = (f32[32]{0:T(128)}, f32[32,1024]{1,0:T(8,128)}) fusion(f32[32,1024]{1,0:T(8,128)} %copy-done.6, f32[32]{0:T(128)} %copy-done.20, f32[1024]{0:T(1024)S(1)} %copy-done.16, bf16[1024,2048]{1,0:T(8,128)(2,1)} %bitcast.102, bf16[1024,2048]{1,0:T(8,128)(2,1)} %bitcast.92, f32[32,2048]{1,0:T(8,128)} %copy-done.12, ...), kind=kOutput, calls=%fused_computation.112 | convolution fusion | flops 269156320 | bytes 8982784 | tf_op jit(solution)/shard_map/dot_general | solution.py:23
  189.1 1.7 convert_dynamic-update-slice_fusion.4
  190.8 7.2 %multiply_reduce_fusion.7 = (f32[32]{0:T(128)}, f32[32,1024]{1,0:T(8,128)}) fusion(f32[32,1024]{1,0:T(8,128)S(1)} %copy-done.5, f32[32]{0:T(128)S(1)} %copy-done.27, f32[1024]{0:T(1024)S(1)} %copy-done.16, bf16[1024,2048]{1,0:T(8,128)(2,1)} %bitcast.103, bf16[1024,2048]{1,0:T(8,128)(2,1)} %bitcast.93, f32[32,2048]{1,0:T(8,128)} %copy-done.11, ...), kind=kOutput, calls=%fused_computation.110 | convolution fusion | flops 269221856 | bytes 9179776 | tf_op jit(solution)/shard_map/dot_general | solution.py:23
  198.6 1.8 convert_dynamic-update-slice_fusion.3
  200.4 7.0 %multiply_reduce_fusion.6 = (f32[32]{0:T(128)}, f32[32,1024]{1,0:T(8,128)}) fusion(f32[32,1024]{1,0:T(8,128)S(1)} %get-tuple-element.28, f32[32]{0:T(128)S(1)} %copy-done.25, f32[1024]{0:T(1024)S(1)} %copy-done.16, bf16[1024,2048]{1,0:T(8,128)(2,1)} %bitcast.104, bf16[1024,2048]{1,0:T(8,128)(2,1)} %bitcast.94, f32[32,2048]{1,0:T(8,128)} %copy-done.10, ...), kind=kOutput, calls=%fused_computation.108 | convolution fusion | flops 269221856 | bytes 9179776 | tf_op jit(solution)/shard_map/dot_general | solution.py:23
  208.1 1.7 convert_dynamic-update-slice_fusion.2
  209.7 6.5 %multiply_reduce_fusion.5 = (f32[32]{0:T(128)S(1)}, f32[32,1024]{1,0:T(8,128)}) fusion(f32[32,1024]{1,0:T(8,128)S(1)} %get-tuple-element.26, f32[32]{0:T(128)S(1)} %copy-done.23, f32[1024]{0:T(1024)S(1)} %copy-done.16, bf16[1024,2048]{1,0:T(8,128)(2,1)} %bitcast.105, bf16[1024,2048]{1,0:T(8,128)(2,1)} %bitcast.95, f32[32,2048]{1,0:T(8,128)} %copy-done.9, ...), kind=kOutput, calls=%fused_computation.106 | convolution fusion | flops 269221856 | bytes 9179776 | tf_op jit(solution)/shard_map/dot_general | solution.py:23
  216.2 1.6 convert_dynamic-update-slice_fusion.1
  217.8 5.7 %multiply_reduce_fusion.4 = (f32[32]{0:T(128)S(1)}, f32[32,1024]{1,0:T(8,128)S(1)}) fusion(f32[32,1024]{1,0:T(8,128)S(1)} %get-tuple-element.24, f32[32]{0:T(128)S(1)} %copy-done.19, f32[1024]{0:T(1024)S(1)} %copy-done.16, bf16[1024,2048]{1,0:T(8,128)(2,1)} %bitcast.106, bf16[1024,2048]{1,0:T(8,128)(2,1)} %bitcast.96, f32[32,2048]{1,0:T(8,128)} %copy-done.8, ...), kind=kOutput, calls=%fused_computation.104 | convolution fusion | flops 269221856 | bytes 9179776 | tf_op jit(solution)/shard_map/dot_general | solution.py:23
  226.7 10.2 %all-to-all-start.2 = ((bf16[128,16,128]{2,1,0:T(8,128)(2,1)}), bf16[128,16,128]{2,1,0:T(8,128)(2,1)S(1)}, u32[]{:S(2)}, u32[]{:S(2)}) async-start(bf16[128,16,128]{2,1,0:T(8,128)(2,1)} %convert_element_type.195), calls=%async_computation.2 | async-start | bytes 1048576 | tf_op jit(solution)/shard_map/all_to_all | solution.py:77
  238.5 1.5 convolution_convert_fusion.1
  241.4 15.7 %all-to-all-done.2 = bf16[128,16,128]{2,1,0:T(8,128)(2,1)S(1)} async-done(((bf16[128,16,128]{2,1,0:T(8,128)(2,1)}), bf16[128,16,128]{2,1,0:T(8,128)(2,1)S(1)}, u32[]{:S(2)}, u32[]{:S(2)}) %all-to-all-start.2) | async-done | bytes 524320 | tf_op jit(solution)/shard_map/all_to_all | solution.py:77
  257.1 5.8 %all-to-all-start.1 = ((bf16[128,8,384]{2,1,0:T(8,128)(2,1)}), bf16[128,8,384]{2,1,0:T(8,128)(2,1)S(1)}, u32[]{:S(2)}, u32[]{:S(2)}) async-start(bf16[128,8,384]{2,1,0:T(8,128)(2,1)} %copy.29), calls=%async_computation.1 | async-start | bytes 1572864 | tf_op jit(solution)/shard_map/all_to_all | solution.py:77
  263.1 25.6 %all-to-all-done.1 = bf16[128,8,384]{2,1,0:T(8,128)(2,1)S(1)} async-done(((bf16[128,8,384]{2,1,0:T(8,128)(2,1)}), bf16[128,8,384]{2,1,0:T(8,128)(2,1)S(1)}, u32[]{:S(2)}, u32[]{:S(2)}) %all-to-all-start.1) | async-done | bytes 786464 | tf_op jit(solution)/shard_map/all_to_all | solution.py:77
  288.9 14.8 %psum.7 = f32[40,128]{1,0:T(8,128)S(1)} all-reduce(f32[40,128]{1,0:T(8,128)S(1)} %pad_maximum_fusion.1), channel_id=1, replica_groups={{0,1,2,3},{4,5,6,7},{8,9,10,11},{12,13,14,15},{16,17,18,19},{20,21,22,2..., use_global_device_ids=true, to_apply=%region_20.21 | all-reduce | flops 5120 | bytes 40960 | tf_op jit(solution)/shard_map/psum | solution.py:170
  (169 shorter events, 40.2 us)
Async XLA Ops:
  7.2 58.3 %copy-start.3 = (bf16[256,1024]{1,0:T(8,128)(2,1)S(1)}, bf16[256,1024]{1,0:T(8,128)(2,1)}, u32[]{:S(2)}) copy-start(bf16[256,1024]{1,0:T(8,128)(2,1)} %param.20) | copy-start | bytes 1572868
  7.2 146.6 %all-gather.2.cloned.1.call-start = ((), (), s32[]{:S(2)}) async-start(), calls=%async_computation.3 | async-start | bytes 8404992 | tf_op jit(solution)/shard_map/all_gather | solution.py:68
  13.1 18.7 %collective-permute-start = (bf16[32,8,1024]{2,1,0:T(8,128)(2,1)S(1)}, bf16[32,8,1024]{2,1,0:T(8,128)(2,1)}, u32[]{:S(2)}, u32[]{:S(2)}) collective-permute-start(bf16[32,8,1024]{2,1,0:T(8,128)(2,1)S(1)} %fusion.11), channel_id=1, source_target_pairs={{0,0},{1,4},{2,8},{3,12},{4,1},{5,5},{6,9},{7,13},{8,2},{9,6},{10,... | collective-permute-start | bytes 1572872 | tf_op jit(solution)/shard_map/ppermute | solution.py:57
  31.8 31.7 %all-to-all-start = ((bf16[32,8,1024]{2,1,0:T(8,128)(2,1)}), bf16[32,8,1024]{2,1,0:T(8,128)(2,1)S(1)}, u32[]{:S(2)}, u32[]{:S(2)}) async-start(bf16[32,8,1024]{2,1,0:T(8,128)(2,1)} %collective-permute-done), calls=%async_computation | async-start | bytes 1048576 | tf_op jit(solution)/shard_map/all_to_all | solution.py:59
  47.3 18.4 %copy-start.17 = (pred[160,256]{1,0:T(8,128)(4,1)}, pred[160,256]{1,0:T(8,128)(4,1)S(1)}, u32[]{:S(2)}) copy-start(pred[160,256]{1,0:T(8,128)(4,1)S(1)} %constant_dynamic-update-slice_fusion) | copy-start | bytes 122884
  64.7 93.0 %copy-start.13 = (bf16[6,32,1024]{2,1,0:T(8,128)(2,1)}, bf16[6,32,1024]{2,1,0:T(8,128)(2,1)S(1)}, u32[]{:S(2)}) copy-start(bf16[6,32,1024]{2,1,0:T(8,128)(2,1)S(1)} %get-tuple-element.17) | copy-start | bytes 1179652
  65.8 92.0 %copy-start.18 = (f32[32]{0:T(128)}, f32[32]{0:T(128)S(1)}, u32[]{:S(2)}) copy-start(f32[32]{0:T(128)S(1)} %add_rsqrt_fusion.6) | copy-start | bytes 388
  157.8 10.5 %copy-start.2 = (bf16[1,128,8,4,512]{4,2,0,3,1:T(8,128)(2,1)}, bf16[1,128,8,4,512]{4,2,0,3,1:T(8,128)(2,1)S(1)}, u32[]{:S(2)}) copy-start(bf16[1,128,8,4,512]{4,2,0,3,1:T(8,128)(2,1)S(1)} %get-tuple-element.21) | copy-start | bytes 12582916
  157.8 11.4 %copy-start.1 = (bf16[1,128,8,4,512]{4,2,0,3,1:T(8,128)(2,1)}, bf16[1,128,8,4,512]{4,2,0,3,1:T(8,128)(2,1)S(1)}, u32[]{:S(2)}) copy-start(bf16[1,128,8,4,512]{4,2,0,3,1:T(8,128)(2,1)S(1)} %get-tuple-element.20) | copy-start | bytes 12582916
  170.6 6.3 %copy-start.33 = (f32[192]{0:T(256)S(1)}, f32[192]{0:T(256)}, u32[]{:S(2)}) copy-start(f32[192]{0:T(256)} %mul.447) | copy-start | bytes 2308
  170.6 7.6 %copy-start.32 = (f32[1024]{0:T(1024)S(1)}, f32[1024]{0:T(1024)}, u32[]{:S(2)}) copy-start(f32[1024]{0:T(1024)} %convert_element_type.178) | copy-start | bytes 12292
  172.2 7.8 %copy-start.7 = (f32[192,1024]{1,0:T(8,128)}, f32[192,1024]{1,0:T(8,128)S(1)}, u32[]{:S(2)}) copy-start(f32[192,1024]{1,0:T(8,128)S(1)} %get-tuple-element.19) | copy-start | bytes 2359300
  174.5 5.5 %copy-start.28 = (f32[192]{0:T(256)}, f32[192]{0:T(256)S(1)}, u32[]{:S(2)}) copy-start(f32[192]{0:T(256)S(1)} %get-tuple-element.41) | copy-start | bytes 2308
  181.4 7.7 %copy-start.21 = (f32[32]{0:T(128)S(1)}, f32[32]{0:T(128)}, u32[]{:S(2)}) copy-start(f32[32]{0:T(128)} %copy-done.20) | copy-start | bytes 388
  181.4 9.5 %copy-start.5 = (f32[32,1024]{1,0:T(8,128)S(1)}, f32[32,1024]{1,0:T(8,128)}, u32[]{:S(2)}) copy-start(f32[32,1024]{1,0:T(8,128)} %copy-done.4) | copy-start | bytes 393220
  181.4 9.4 %copy-start.27 = (f32[32]{0:T(128)S(1)}, f32[32]{0:T(128)}, u32[]{:S(2)}) copy-start(f32[32]{0:T(128)} %copy-done.26) | copy-start | bytes 388
  190.8 9.6 %copy-start.25 = (f32[32]{0:T(128)S(1)}, f32[32]{0:T(128)}, u32[]{:S(2)}) copy-start(f32[32]{0:T(128)} %copy-done.24) | copy-start | bytes 388
  200.4 7.7 %copy-start.14 = (f32[32,1024]{1,0:T(8,128)S(1)}, f32[32,1024]{1,0:T(8,128)}, u32[]{:S(2)}) copy-start(f32[32,1024]{1,0:T(8,128)} %get-tuple-element.13) | copy-start | bytes 393220
  200.4 9.3 %copy-start.23 = (f32[32]{0:T(128)S(1)}, f32[32]{0:T(128)}, u32[]{:S(2)}) copy-start(f32[32]{0:T(128)} %copy-done.22) | copy-start | bytes 388
  209.7 6.5 %copy-start.15 = (f32[32,1024]{1,0:T(8,128)S(1)}, f32[32,1024]{1,0:T(8,128)}, u32[]{:S(2)}) copy-start(f32[32,1024]{1,0:T(8,128)} %get-tuple-element.11) | copy-start | bytes 393220
  209.7 8.1 %copy-start.19 = (f32[32]{0:T(128)S(1)}, f32[32]{0:T(128)}, u32[]{:S(2)}) copy-start(f32[32]{0:T(128)} %copy-done.18) | copy-start | bytes 388
  223.6 14.9 %copy-start.29 = (f32[192]{0:T(256)S(1)}, f32[192]{0:T(256)}, u32[]{:S(2)}) copy-start(f32[192]{0:T(256)} %copy-done.28) | copy-start | bytes 2308
  226.7 30.4 %all-to-all-start.2 = ((bf16[128,16,128]{2,1,0:T(8,128)(2,1)}), bf16[128,16,128]{2,1,0:T(8,128)(2,1)S(1)}, u32[]{:S(2)}, u32[]{:S(2)}) async-start(bf16[128,16,128]{2,1,0:T(8,128)(2,1)} %convert_element_type.195), calls=%async_computation.2 | async-start | bytes 1048576 | tf_op jit(solution)/shard_map/all_to_all | solution.py:77
  257.1 31.6 %all-to-all-start.1 = ((bf16[128,8,384]{2,1,0:T(8,128)(2,1)}), bf16[128,8,384]{2,1,0:T(8,128)(2,1)S(1)}, u32[]{:S(2)}, u32[]{:S(2)}) async-start(bf16[128,8,384]{2,1,0:T(8,128)(2,1)} %copy.29), calls=%async_computation.1 | async-start | bytes 1572864 | tf_op jit(solution)/shard_map/all_to_all | solution.py:77
  (18 other events, 46.4 us)
Sparse Core Ops, SparseCore 0:
  12.5 141.2 all-gather.1

commit v2 on v1

v2 whole, which is shorter than its diff:
```python
import functools
import jax
import jax.numpy as jnp
from jax import lax
from jax.experimental import pallas as pl
from jax.experimental.pallas import tpu as pltpu
from jax.sharding import PartitionSpec as P

discount = 0.997
epsilon = 1e-06
f32 = jnp.float32
bf16 = jnp.bfloat16


def dot_nn(a, b):
    return lax.dot_general(a, b, (((1,), (0,)), ((), ())), preferred_element_type=f32)


def dot_nt(a, b):
    return lax.dot_general(a, b, (((1,), (1,)), ((), ())), preferred_element_type=f32)


def inverse_scale(vector):
    return lax.rsqrt(jnp.mean(vector * vector, axis=-1, keepdims=True) + epsilon)


def norm_back(vector, upstream, gain):
    factor = inverse_scale(vector)
    unit_vec = vector * factor
    scaled = upstream * gain
    return factor * (scaled - unit_vec * jnp.mean(scaled * unit_vec, axis=-1, keepdims=True))


def block_kernel(
    steps, share, half, nblocks, arrays, pieces,
    core_ref, obs_ref, emb_ref, keys_ref, targets_ref, value_targets_ref, weight_ref, w_pol_ref,
    w_val_ref, gain_ref, *rest,
):
    hbm = rest[:arrays]
    mine_ref, other_ref = rest[arrays:arrays + 2]
    weights, latents, mixeds, preacts, lows, head_sums, sems = rest[arrays + 2:]
    chips = mine_ref.shape[0]
    core = core_ref[0]
    width = lows.shape[1]
    parts = lows.shape[0] // (steps * share)
    copies = []
    for j, (array, start) in enumerate(pieces):
        source = hbm[array].at[pl.ds(start, weights.shape[1]), :]
        copies.append(pltpu.make_async_copy(source, weights.at[j], sems.at[j]))
        copies[j].start()
    gain = gain_ref[...]

    def rows_of(position):
        return pl.ds(pl.multiple_of(position * share, share), share)

    def forward(position, latent):
        here = rows_of(position)
        mixed = latent + emb_ref[here, :].astype(f32)
        mixeds[here, :] = mixed
        normed = (mixed * inverse_scale(mixed) * gain).astype(bf16)
        total = jnp.zeros_like(mixed)
        for j in range(nblocks):
            @pl.when(position == 0)
            def _():
                copies[j].wait()
            preact = dot_nn(normed, weights[j, :, :half])
            preacts[here, j * half:(j + 1) * half] = preact
            hidden = (preact / (1.0 + jnp.exp(-preact))).astype(bf16)
            total = total + dot_nt(hidden, weights[j, :, half:])
        latent = mixed + total
        latents[rows_of(position + 1), :] = latent
        return latent

    first = obs_ref[...].astype(f32)
    latents[:share, :] = first
    lax.fori_loop(0, steps, forward, first)

    stacked = latents[...]
    scale = inverse_scale(stacked)
    head_in = (stacked * scale * gain).astype(bf16)
    logits = dot_nn(head_in, w_pol_ref[...])
    w_val = w_val_ref[...].astype(f32)
    values = jnp.sum(head_in.astype(f32) * w_val, axis=-1, keepdims=True)
    weight = weight_ref[...]
    exped = jnp.exp(logits - jnp.max(logits, axis=-1, keepdims=True))
    probs = exped / jnp.sum(exped, axis=-1, keepdims=True)
    logit_grad = (weight * (probs - targets_ref[...])).astype(bf16)
    value_grad = 2.0 * weight * (values - value_targets_ref[...])
    high = value_grad.astype(bf16)
    low = (value_grad - high.astype(f32)).astype(bf16)
    lane = lax.broadcasted_iota(jnp.int32, (value_grad.shape[0], 128), 1)
    value_lanes = jnp.where(lane == 0, high, jnp.where(lane == 1, low, jnp.zeros_like(low)))
    head_grads = jnp.concatenate([logit_grad, value_lanes], axis=1)
    sums = lax.dot_general(
        head_in, head_grads, (((0,), (0,)), ((), ())), preferred_element_type=f32
    )
    head_sums[...] = sums.reshape(head_sums.shape)
    columns = sums.shape[1]
    mine_ref[:, :, :columns] = head_sums[:, core]
    other_ref[:, :, :columns] = head_sums[:, 1 - core].astype(bf16)
    head_grad = dot_nt(logit_grad, w_pol_ref[...]) + value_grad * w_val
    unit_vec = stacked * scale
    scaled = head_grad * gain
    latents[...] = scale * (scaled - unit_vec * jnp.mean(scaled * unit_vec, axis=-1, keepdims=True))

    def backward(index, cotangent):
        position = steps - 1 - index
        here = rows_of(position)
        low = cotangent.astype(bf16)
        total = jnp.zeros_like(cotangent)
        for j in range(nblocks):
            hidden_grad = dot_nn(low, weights[j, :, half:])
            preact = preacts[here, j * half:(j + 1) * half]
            sig = 1.0 / (1.0 + jnp.exp(-preact))
            preact_grad = (hidden_grad * sig * (1.0 + preact * (1.0 - sig))).astype(bf16)
            total = total + dot_nt(preact_grad, weights[j, :, :half])
        mixed_grad = cotangent + norm_back(mixeds[here, :], total, gain)
        mixed_low = mixed_grad.astype(bf16)
        for quarter in range(parts):
            start = pl.multiple_of(quarter * steps * share + position * share, share)
            lows[pl.ds(start, share), :] = mixed_low[:, quarter * width:(quarter + 1) * width]
        return mixed_grad + latents[here, :]

    lax.fori_loop(0, steps, backward, latents[steps * share:, :])

    row = lax.broadcasted_iota(jnp.int32, (chips * 8, keys_ref.shape[1]), 0)
    row_key = 2 * row - (row & 7)
    for side, target in ((core, mine_ref), (1 - core, other_ref)):
        picks = jnp.where(row_key + 8 * side == keys_ref[...], 1.0, 0.0).astype(bf16)
        summed = dot_nn(picks, lows[...]).reshape(chips, 8, width)
        target[:, :, columns:] = summed.astype(target.dtype)


def run_block(
    core, obs0, emb, actions, targets, value_targets, weight, w_pol, w_val, gain, blocks, chips
):
    share, features = obs0.shape
    steps = emb.shape[0] // share
    num_actions = w_pol.shape[1]
    parts = 8 * chips * 2 // num_actions
    width = features // parts
    columns = num_actions + 128 + width
    quarters = jnp.arange(parts, dtype=jnp.int32)
    keys = (actions.reshape(1, -1) * parts + quarters[:, None]).reshape(1, -1)
    nblocks = sum(block.shape[0] for block in blocks) // features
    half = blocks[0].shape[1] // 2
    rows = (steps + 1) * share
    pieces = [
        (i, k * features) for i, block in enumerate(blocks) for k in range(block.shape[0] // features)
    ]
    vmem = pl.BlockSpec(memory_space=pltpu.VMEM)
    return pl.pallas_call(
        functools.partial(block_kernel, steps, share, half, nblocks, len(blocks), tuple(pieces)),
        out_shape=(
            jax.ShapeDtypeStruct((chips, 8, columns), f32),
            jax.ShapeDtypeStruct((chips, 8, columns), bf16),
        ),
        in_specs=[pl.BlockSpec(memory_space=pltpu.SMEM)]
        + [vmem] * 9
        + [pl.BlockSpec(memory_space=pltpu.HBM)] * len(blocks),
        out_specs=(vmem,) * 2,
        scratch_shapes=[
            pltpu.VMEM((nblocks, features, 2 * half), bf16),
            pltpu.VMEM((rows, features), f32),
            pltpu.VMEM((steps * share, features), f32),
            pltpu.VMEM((steps * share, nblocks * half), f32),
            pltpu.VMEM((parts * steps * share, width), bf16),
            pltpu.VMEM((chips, 2, 8, num_actions + 128), f32),
            pltpu.SemaphoreType.DMA((nblocks,)),
        ],
        compiler_params=pltpu.CompilerParams(vmem_limit_bytes=40 * 1024 * 1024),
        cost_estimate=pl.CostEstimate(flops=3 * 10**9, bytes_accessed=10**7, transcendentals=0),
    )(core, obs0, emb, keys, targets, value_targets, weight, w_pol, w_val, gain, *blocks)


def cores_swap(value, tables):
    return lax.ppermute(value, "table", [(t, t ^ 1) for t in range(tables)])


def along_x(value, step, members):
    return lax.ppermute(value, "mp", [(m, (m + step) % members) for m in range(members)])


def same_core_groups(tables):
    return [[2 * k + c for k in range(tables // 2)] for c in range(2)]


def own_rows_of_weights(w_in, w_out, core, tables):
    half = w_in.shape[1] // 2
    low = jnp.concatenate([w_in[:, :half], w_out[:, :half]], axis=1)
    high = jnp.concatenate([w_in[:, half:], w_out[:, half:]], axis=1)
    first = core == 0
    mine = jnp.where(first, low, high)
    got = cores_swap(jnp.where(first, high, low), tables)
    return jnp.where(
        first, jnp.concatenate([mine, got], axis=0), jnp.concatenate([got, mine], axis=0)
    )


def gather_plane(rows, tables):
    return lax.all_to_all(
        jnp.tile(rows, (tables // 2, 1)),
        "table",
        split_axis=0,
        concat_axis=0,
        tiled=True,
        axis_index_groups=same_core_groups(tables),
    )


def gather_blocks(own, tables, members):
    groups = [
        [(2 * k + c) * members + m for c in range(2) for m in range(members)]
        for k in range(tables // 2)
    ]
    return [lax.all_gather(own, ("table", "mp"), axis=0, tiled=True, axis_index_groups=groups)]


def pick_unrolls(replay, request_rows, request_count, steps, member, tables, members):
    share = tables // members
    width = replay.shape[1]
    firsts = request_rows[0, :, 0].reshape(share, members)
    firsts = lax.dynamic_index_in_dim(firsts, member, 1, keepdims=False)
    counts = lax.dynamic_index_in_dim(
        request_count[0].reshape(share, members), member, 1, keepdims=False
    )
    used = (counts > 0).astype(f32)
    offsets = jnp.arange(8, dtype=jnp.int32)
    positions = firsts[:, None] + offsets[None, :]
    row_ids = jnp.arange(replay.shape[0], dtype=jnp.int32)
    picks = (positions.reshape(-1)[:, None] == row_ids[None, :]).astype(bf16)
    rows = jnp.dot(picks, replay, preferred_element_type=f32).reshape(share, 8, width)
    rows = jnp.where(offsets[None, :, None] <= steps, rows, used[:, None, None])
    return rows.astype(bf16)


def swap_digits(rows, tables, members):
    share = tables // members
    swap = [
        ((members * a + b) * members + d, (members * a + d) * members + b)
        for a in range(share)
        for b in range(members)
        for d in range(members)
    ]
    return lax.ppermute(rows, ("table", "mp"), swap)


def deliver_unrolls(rows, tables, members):
    share = tables // members
    groups = [[members * a + d for a in range(share)] for d in range(members)]
    return lax.all_to_all(
        rows, "table", split_axis=0, concat_axis=0, tiled=True, axis_index_groups=groups
    )


def reduce_partials(mine, other, tables, members):
    got = cores_swap(other, tables)
    summed = (mine + got.astype(f32)).astype(bf16)
    parts = lax.all_to_all(
        summed,
        "table",
        split_axis=0,
        concat_axis=0,
        tiled=True,
        axis_index_groups=same_core_groups(tables),
    )
    summed = jnp.sum(parts.astype(f32), axis=0)
    copies = jnp.broadcast_to(summed[None], (members, *summed.shape))
    return jnp.sum(lax.all_to_all(copies, "mp", split_axis=0, concat_axis=0, tiled=True), axis=0)


def per_device(
    replay, request_rows, request_count, actions, rewards, w_in, w_out, w_pol, w_val, embed, gain
):
    tables = lax.axis_size("table")
    members = lax.axis_size("mp")
    member = lax.axis_index("mp")
    core = lax.axis_index("table") % 2
    share = tables // members
    features = replay.shape[1]
    steps = actions.shape[0]
    num_actions = w_pol.shape[1]
    own_rows = own_rows_of_weights(w_in, w_out, core, tables)
    rows = pick_unrolls(replay, request_rows, request_count, steps, member, tables, members)
    own = gather_plane(own_rows, tables)
    blocks = gather_blocks(own, tables, members)
    rows, _ = lax.optimization_barrier((rows, own))
    rows = swap_digits(rows, tables, members)
    rows = deliver_unrolls(rows, tables, members)
    observed = rows[:, : steps + 1].transpose(1, 0, 2)
    used_rows = rows[:, steps + 1, 0].astype(f32)
    actions = lax.dynamic_index_in_dim(
        actions.reshape(steps, share, members), member, 2, keepdims=False
    )
    rewards = lax.dynamic_index_in_dim(
        rewards.reshape(steps, share, members), member, 2, keepdims=False
    )
    flat_obs = observed.reshape((steps + 1) * share, features).astype(f32)
    target_in = (flat_obs * inverse_scale(flat_obs) * gain).astype(bf16)
    target_logits = jnp.dot(target_in, w_pol, preferred_element_type=f32)
    target_values = jnp.dot(target_in, w_val, preferred_element_type=f32).reshape(
        steps + 1, share
    )
    policy_targets = jax.nn.softmax(target_logits, axis=-1)
    value_targets = jnp.concatenate(
        [rewards + discount * target_values[1:], target_values[steps:]], axis=0
    )
    action_ids = jnp.arange(num_actions, dtype=jnp.int32)
    onehots = (actions.reshape(-1)[:, None] == action_ids[None, :]).astype(bf16)
    emb = jnp.dot(onehots, embed, preferred_element_type=f32).astype(bf16)
    row_weight = jnp.tile(used_rows / tables, steps + 1)
    mine, other = run_block(
        core.reshape(1),
        observed[0],
        emb,
        actions,
        policy_targets,
        value_targets.reshape(-1, 1),
        row_weight[:, None],
        w_pol,
        w_val[None, :],
        gain[None, :],
        blocks,
        tables // 2,
    )
    rows = reduce_partials(mine, other, tables, members)
    out_pol = rows[:, :num_actions]
    out_val = rows[:, num_actions] + rows[:, num_actions + 1]
    out_embed = rows[:, num_actions + 128 :].reshape(num_actions // tables, features)
    return out_pol, out_embed, out_val


def solution(mesh):
    return jax.shard_map(
        per_device,
        mesh=mesh,
        in_specs=(
            P("table", None),
            P("table", None, None),
            P("table", None),
            P(None, "table"),
            P(None, "table"),
            P("table", "mp"),
            P("table", "mp"),
            P(),
            P(),
            P(),
            P(),
        ),
        out_specs=(P("table", None), P("table", None), P("table")),
        check_vma=False,
    )
```

time: 313 us -> 202 us (0.65)
  waiting for transfers between devices: 155 us -> 42.1 us
  blocking collectives: 14.8 us -> 84.7 us
  matrix products: 55.7 us -> 1.34 us
  Pallas kernels: 0 us -> 32.5 us
  starting transfers between devices: 36 us -> 15.2 us
  other arithmetic: 21 us -> 3.86 us
  local copies, waits for them, and re-layouts: 14.8 us -> 7.89 us
    all_to_all x0 -> x3, blocking collectives: none -> 84.7 us  [the longest x1 46.3 us: gather_plane(): lax.all_to_all(jnp.tile(rows, (tables // 2, 1)), 'table', split_axis=0, c...]
    all_gather x1, waiting for transfers between devices: 87.9 us -> 9.09 us  [gather_blocks(): lax.all_gather(own, ('table', 'mp'), axis=0, tiled=True, axis_index_group...]
    dot_general x28 -> x4, matrix products: 55.7 us -> 1.34 us  [the longest x1 0.49 us: pick_unrolls(): jnp.dot(picks, replay, preferred_element_type=f32).reshape(share, 8, width)]
    all_to_all x3 -> x1, waiting for transfers between devices: 57.5 us -> 15 us  [deliver_unrolls(): lax.all_to_all(rows, 'table', split_axis=0, concat_axis=0, tiled=True, ax...]
    pallas_call x0 -> x1, Pallas kernels: none -> 32.5 us  [run_block(): pl.pallas_call(functools.partial(block_kernel, steps, share, half, nblock...]
    all_to_all x3 -> x1, starting transfers between devices: 31.1 us -> 6.01 us  [deliver_unrolls(): lax.all_to_all(rows, 'table', split_axis=0, concat_axis=0, tiled=True, ax...]
    psum x1 -> x0, blocking collectives: 14.8 us -> none  [per_device(): packed = lax.psum(packed, ('table', 'mp'), axis_index_groups=lines)]
    unnamed x11 -> x2, other arithmetic: 9.75 us -> 1.33 us
  transfers between devices with their start and end apart: 5 -> 5, of which waited for: 5 -> 5; matrix products, arithmetic and copies ran while one was open for 5% -> 3% of each run, Pallas kernels for 0% -> 0%
where the time goes in v2:
time: 202 us
  blocking collectives  84.7 us (42%)
  waiting for transfers between devices  42.1 us (21%)
  Pallas kernels  32.5 us (16%)
  starting transfers between devices  15.2 us (8%)
  between operations  14.4 us (7%)
  local copies, waits for them, and re-layouts  7.89 us (4%)
  other arithmetic  3.86 us (2%)
    all_to_all x1, blocking collectives, gather_plane(): lax.all_to_all(jnp.tile(rows, (tables // 2, 1)), 'table', split_axis=0, c...  46.3 us
    pallas_call x1, Pallas kernels, run_block(): pl.pallas_call(functools.partial(block_kernel, steps, share, half, nblock...  32.5 us
    all_to_all x1, blocking collectives, reduce_partials(): lax.all_to_all(summed, 'table', split_axis=0, concat_axis=0, tiled=True,...  29.3 us
    ppermute x1, waiting for transfers between devices, swap_digits(): return lax.ppermute(rows, ('table', 'mp'), swap)  15.1 us
    all_to_all x1, waiting for transfers between devices, deliver_unrolls(): lax.all_to_all(rows, 'table', split_axis=0, concat_axis=0, tiled=True, ax...  15 us
    all_to_all x1, blocking collectives, reduce_partials(): lax.all_to_all(copies, 'mp', split_axis=0, concat_axis=0, tiled=True)  9.17 us
    all_gather x1, waiting for transfers between devices, gather_blocks(): lax.all_gather(own, ('table', 'mp'), axis=0, tiled=True, axis_index_group...  9.09 us
    all_to_all x1, starting transfers between devices, deliver_unrolls(): lax.all_to_all(rows, 'table', split_axis=0, concat_axis=0, tiled=True, ax...  6.01 us
  transfers between devices with their start and end apart: 5, of which 5 were waited for; matrix products, arithmetic and copies ran while one was open for 3% of the time, Pallas kernels for 0%

profile of v2, /device:TPU:8, one launch (start us, length us, event | category | flops | bytes accessed | tf_op | source)
XLA Modules:
  0.0 202.0 jit_solution(16348622891646386115)
XLA Ops:
  7.2 0.8 fusion.12
  8.1 1.9 collective-permute-start
  10.0 1.1 collective-permute-done
  11.3 46.3 %all_to_all.24 = bf16[64,16,512]{2,1,0:T(8,128)(2,1)} all-to-all(bf16[64,16,512]{2,1,0:T(8,128)(2,1)S(1)} %tile.4), channel_id=1, replica_groups={{0,8,16,24,32,40,48,56,64,72,80,88,96,104,112,120,128,136,144,152,160,1..., dimensions={0} | all-to-all | bytes 2097152 | tf_op jit(solution)/shard_map/all_to_all | solution.py:201
  57.6 0.5 broadcast.79
  58.1 0.7 reduce.20
  58.8 0.7 reduce.19
  60.2 0.5 fusion.1
  60.7 5.1 %collective-permute-start.1 = (bf16[32,8,1024]{2,1,0:T(8,128)(2,1)S(1)}, bf16[32,8,1024]{2,1,0:T(8,128)(2,1)}, u32[]{:S(2)}, u32[]{:S(2)}) collective-permute-start(bf16[32,8,1024]{2,1,0:T(8,128)(2,1)S(1)} %fusion.1), channel_id=1, source_target_pairs={{0,0},{1,4},{2,8},{3,12},{4,1},{5,5},{6,9},{7,13},{8,2},{9,6},{10,... | collective-permute-start | bytes 1572872 | tf_op jit(solution)/shard_map/ppermute | solution.py:245
  65.8 15.1 %collective-permute-done.1 = bf16[32,8,1024]{2,1,0:T(8,128)(2,1)} collective-permute-done((bf16[32,8,1024]{2,1,0:T(8,128)(2,1)S(1)}, bf16[32,8,1024]{2,1,0:T(8,128)(2,1)}, u32[]{:S(2)}, u32[]{:S(2)}) %collective-permute-start.1) | collective-permute-done | bytes 524320 | tf_op jit(solution)/shard_map/ppermute | solution.py:245
  81.0 6.0 %all-to-all-start.1 = ((bf16[32,8,1024]{2,1,0:T(8,128)(2,1)}), bf16[32,8,1024]{2,1,0:T(8,128)(2,1)S(1)}, u32[]{:S(2)}, u32[]{:S(2)}) async-start(bf16[32,8,1024]{2,1,0:T(8,128)(2,1)} %collective-permute-done.1), calls=%async_computation.1 | async-start | bytes 1048576 | tf_op jit(solution)/shard_map/all_to_all | solution.py:251
  88.2 15.0 %all-to-all-done.1 = bf16[32,8,1024]{2,1,0:T(8,128)(2,1)S(1)} async-done(((bf16[32,8,1024]{2,1,0:T(8,128)(2,1)}), bf16[32,8,1024]{2,1,0:T(8,128)(2,1)S(1)}, u32[]{:S(2)}, u32[]{:S(2)}) %all-to-all-start.1) | async-done | bytes 524320 | tf_op jit(solution)/shard_map/all_to_all | solution.py:251
  103.6 0.3 multiply_reduce_fusion
  104.8 0.4 fusion.14
  105.5 9.1 %all-gather.2.cloned.1.call-done.rest_0_ = bf16[8192,512]{1,0:T(8,128)(2,1)} async-done(((bf16[1024,512]{1,0:T(8,128)(2,1)}), bf16[8192,512]{1,0:T(8,128)(2,1)}) %all-gather.2.cloned.1.call-update) | async-done | bytes 8388624 | tf_op jit(solution)/shard_map/all_gather | solution.py:216
  114.6 3.4 %copy-done.3 = bf16[8192,512]{1,0:T(8,128)(2,1)S(1)} copy-done((bf16[8192,512]{1,0:T(8,128)(2,1)S(1)}, bf16[8192,512]{1,0:T(8,128)(2,1)}, u32[]{:S(2)}) %copy-start.3) | copy-done | bytes 8388632
  118.0 32.5 %shard_map.130 = (f32[64,8,640]{2,1,0:T(8,128)S(1)}, bf16[64,8,640]{2,1,0:T(8,128)(2,1)S(1)}) custom-call(s32[1]{0:T(128)} %bitcast.core_ref, bf16[32,1024]{1,0:T(8,128)(2,1)S(1)} %slice_bitcast_fusion.obs_ref, bf16[160,1024]{1,0:T(8,128)(2,1)S(1)} %convolution_convert_fusion.emb_ref, s32[1,640]{1,0:T(1,128)S(1)} %add.92.keys_ref, ...), custom_call_target="tpu_custom_call" | custom-call | flops 3000000000 | bytes 10000000 | tf_op jit(solution)/shard_map/pallas_call | solution.py:152
  150.5 2.2 %collective-permute-start.2 = (bf16[64,8,640]{2,1,0:T(8,128)(2,1)S(1)}, bf16[64,8,640]{2,1,0:T(8,128)(2,1)S(1)}, u32[]{:S(2)}, u32[]{:S(2)}) collective-permute-start(bf16[64,8,640]{2,1,0:T(8,128)(2,1)S(1)} %get-tuple-element.8), channel_id=1, source_target_pairs={{0,4},{4,0},{8,12},{12,8},{16,20},{20,16},{24,28},{28,24},{32,36},... | collective-permute-start | bytes 1966088 | tf_op jit(solution)/shard_map/ppermute | solution.py:177
  152.7 1.8 collective-permute-done.2
  154.6 29.3 %all_to_all.25 = bf16[64,8,640]{2,1,0:T(8,128)(2,1)S(1)} all-to-all(bf16[64,8,640]{2,1,0:T(8,128)(2,1)S(1)} %add_convert_fusion), channel_id=1, replica_groups={{0,8,16,24,32,40,48,56,64,72,80,88,96,104,112,120,128,136,144,152,160,1..., dimensions={0} | all-to-all | bytes 1310720 | tf_op jit(solution)/shard_map/all_to_all | solution.py:259
  184.1 9.2 %all_to_all.26 = f32[4,8,640]{2,1,0:T(8,128)S(1)} all-to-all(f32[4,8,640]{2,1,0:T(8,128)S(1)} %broadcast_in_dim.26), channel_id=1, replica_groups=mesh['table'=128,'mp'=4] {'mp'}, dimensions={0} | all-to-all | bytes 163840 | tf_op jit(solution)/shard_map/all_to_all | solution.py:269
  193.3 0.7 fusion.10
  193.9 0.6 fusion.11
  194.5 0.6 reshape.190
  (62 shorter events, 4.0 us)
Async XLA Ops:
  7.2 53.0 %copy-start = (bf16[512,1024]{1,0:T(8,128)(2,1)S(1)}, bf16[512,1024]{1,0:T(8,128)(2,1)}, u32[]{:S(2)}) copy-start(bf16[512,1024]{1,0:T(8,128)(2,1)} %param.11) | copy-start | bytes 3145732
  7.2 107.4 %all-gather.2.cloned.1.call-start = ((), (), s32[]{:S(2)}) async-start(), calls=%async_computation.4 | async-start | bytes 9437184 | tf_op jit(solution)/shard_map/all_gather | solution.py:216
  8.1 3.1 %collective-permute-start = (bf16[8,512]{1,0:T(8,128)(2,1)S(1)}, bf16[8,512]{1,0:T(8,128)(2,1)S(1)}, u32[]{:S(2)}, u32[]{:S(2)}) collective-permute-start(bf16[8,512]{1,0:T(8,128)(2,1)S(1)} %get-tuple-element.14), channel_id=1, source_target_pairs={{0,4},{4,0},{8,12},{12,8},{16,20},{20,16},{24,28},{28,24},{32,36},... | collective-permute-start | bytes 24584 | tf_op jit(solution)/shard_map/ppermute | solution.py:177
  11.3 46.8 %copy-start.8 = (s32[1,128,1]{1,2,0:T(1,128)S(1)}, s32[1,128,1]{1,2,0:T(1,128)}, u32[]{:S(2)}) copy-start(s32[1,128,1]{1,2,0:T(1,128)} %param.12) | copy-start | bytes 1540
  11.3 47.5 %copy-start.9 = (s32[1,128]{1,0:T(1,128)S(1)}, s32[1,128]{1,0:T(1,128)}, u32[]{:S(2)}) copy-start(s32[1,128]{1,0:T(1,128)} %param.13) | copy-start | bytes 1540
  60.2 26.8 %copy-start.5 = (bf16[1024]{0:T(1024)(128)(2,1)S(1)}, bf16[1024]{0:T(1024)(128)(2,1)}, u32[]{:S(2)}) copy-start(bf16[1024]{0:T(1024)(128)(2,1)} %param.19) | copy-start | bytes 6148
  60.2 26.8 %copy-start.6 = (s32[5,128]{1,0:T(8,128)S(1)}, s32[5,128]{1,0:T(8,128)}, u32[]{:S(2)}) copy-start(s32[5,128]{1,0:T(8,128)} %param.14) | copy-start | bytes 7684
  60.2 27.4 %copy-start.7 = (f32[5,128]{1,0:T(8,128)S(1)}, f32[5,128]{1,0:T(8,128)}, u32[]{:S(2)}) copy-start(f32[5,128]{1,0:T(8,128)} %param.15) | copy-start | bytes 7684
  60.2 27.7 %copy-start.4 = (bf16[256,1024]{1,0:T(8,128)(2,1)S(1)}, bf16[256,1024]{1,0:T(8,128)(2,1)}, u32[]{:S(2)}) copy-start(bf16[256,1024]{1,0:T(8,128)(2,1)} %param.20) | copy-start | bytes 1572868
  60.7 20.2 %collective-permute-start.1 = (bf16[32,8,1024]{2,1,0:T(8,128)(2,1)S(1)}, bf16[32,8,1024]{2,1,0:T(8,128)(2,1)}, u32[]{:S(2)}, u32[]{:S(2)}) collective-permute-start(bf16[32,8,1024]{2,1,0:T(8,128)(2,1)S(1)} %fusion.1), channel_id=1, source_target_pairs={{0,0},{1,4},{2,8},{3,12},{4,1},{5,5},{6,9},{7,13},{8,2},{9,6},{10,... | collective-permute-start | bytes 1572872 | tf_op jit(solution)/shard_map/ppermute | solution.py:245
  81.0 22.2 %all-to-all-start.1 = ((bf16[32,8,1024]{2,1,0:T(8,128)(2,1)}), bf16[32,8,1024]{2,1,0:T(8,128)(2,1)S(1)}, u32[]{:S(2)}, u32[]{:S(2)}) async-start(bf16[32,8,1024]{2,1,0:T(8,128)(2,1)} %collective-permute-done.1), calls=%async_computation.1 | async-start | bytes 1048576 | tf_op jit(solution)/shard_map/all_to_all | solution.py:251
  87.0 17.1 %copy-start.2 = (f32[1024]{0:T(1024)S(1)}, f32[1024]{0:T(1024)}, u32[]{:S(2)}) copy-start(f32[1024]{0:T(1024)} %param.21) | copy-start | bytes 12292
  88.2 16.6 %copy-start.1 = (bf16[1024,256]{1,0:T(8,128)(2,1)S(1)}, bf16[1024,256]{1,0:T(8,128)(2,1)}, u32[]{:S(2)}) copy-start(bf16[1024,256]{1,0:T(8,128)(2,1)} %w_pol_ref.1) | copy-start | bytes 1572868
  114.6 3.4 %copy-start.3 = (bf16[8192,512]{1,0:T(8,128)(2,1)S(1)}, bf16[8192,512]{1,0:T(8,128)(2,1)}, u32[]{:S(2)}) copy-start(bf16[8192,512]{1,0:T(8,128)(2,1)} %all-gather.2.cloned.1.call-done.rest_0_) | copy-start | bytes 25165828
  150.5 4.0 %collective-permute-start.2 = (bf16[64,8,640]{2,1,0:T(8,128)(2,1)S(1)}, bf16[64,8,640]{2,1,0:T(8,128)(2,1)S(1)}, u32[]{:S(2)}, u32[]{:S(2)}) collective-permute-start(bf16[64,8,640]{2,1,0:T(8,128)(2,1)S(1)} %get-tuple-element.8), channel_id=1, source_target_pairs={{0,4},{4,0},{8,12},{12,8},{16,20},{20,16},{24,28},{28,24},{32,36},... | collective-permute-start | bytes 1966088 | tf_op jit(solution)/shard_map/ppermute | solution.py:177
Sparse Core Ops, SparseCore 0:
  57.7 56.8 all-gather.1

commit v3 on v2

--- a/solution.py
+++ b/solution.py
@@ -38,7 +38,7 @@
 ):
     hbm = rest[:arrays]
     mine_ref, other_ref = rest[arrays:arrays + 2]
-    weights, latents, mixeds, preacts, lows, head_sums, sems = rest[arrays + 2:]
+    weights, latents, mixeds, slopes, lows, head_sums, sems = rest[arrays + 2:]
     chips = mine_ref.shape[0]
     core = core_ref[0]
     width = lows.shape[1]
@@ -51,29 +51,33 @@
     gain = gain_ref[...]
 
     def rows_of(position):
-        return pl.ds(pl.multiple_of(position * share, share), share)
-
-    def forward(position, latent):
+        start = position * share
+        return pl.ds(start if isinstance(start, int) else pl.multiple_of(start, share), share)
+
+    def forward(position, latent, arriving=False):
         here = rows_of(position)
         mixed = latent + emb_ref[here, :].astype(f32)
         mixeds[here, :] = mixed
         normed = (mixed * inverse_scale(mixed) * gain).astype(bf16)
-        total = jnp.zeros_like(mixed)
+        hiddens = []
         for j in range(nblocks):
-            @pl.when(position == 0)
-            def _():
+            if arriving:
                 copies[j].wait()
             preact = dot_nn(normed, weights[j, :, :half])
-            preacts[here, j * half:(j + 1) * half] = preact
-            hidden = (preact / (1.0 + jnp.exp(-preact))).astype(bf16)
-            total = total + dot_nt(hidden, weights[j, :, half:])
+            sig = 1.0 / (1.0 + jnp.exp(-preact))
+            slopes[here, j * half:(j + 1) * half] = sig * (1.0 + preact * (1.0 - sig))
+            hiddens.append((preact * sig).astype(bf16))
+        total = jnp.zeros((mixed.shape[1], share), f32)
+        for j in range(nblocks):
+            total = total + dot_nt(weights[j, :, half:], hiddens[j])
+        total = total.T
         latent = mixed + total
         latents[rows_of(position + 1), :] = latent
         return latent
 
     first = obs_ref[...].astype(f32)
     latents[:share, :] = first
-    lax.fori_loop(0, steps, forward, first)
+    lax.fori_loop(1, steps, forward, forward(0, first, arriving=True))
 
     stacked = latents[...]
     scale = inverse_scale(stacked)
@@ -107,13 +111,14 @@
         position = steps - 1 - index
         here = rows_of(position)
         low = cotangent.astype(bf16)
-        total = jnp.zeros_like(cotangent)
+        preact_grads = []
         for j in range(nblocks):
             hidden_grad = dot_nn(low, weights[j, :, half:])
-            preact = preacts[here, j * half:(j + 1) * half]
-            sig = 1.0 / (1.0 + jnp.exp(-preact))
-            preact_grad = (hidden_grad * sig * (1.0 + preact * (1.0 - sig))).astype(bf16)
-            total = total + dot_nt(preact_grad, weights[j, :, :half])
+            preact_grads.append((hidden_grad * slopes[here, j * half:(j + 1) * half]).astype(bf16))
+        total = jnp.zeros((cotangent.shape[1], share), f32)
+        for j in range(nblocks):
+            total = total + dot_nt(weights[j, :, :half], preact_grads[j])
+        total = total.T
         mixed_grad = cotangent + norm_back(mixeds[here, :], total, gain)
         mixed_low = mixed_grad.astype(bf16)
         for quarter in range(parts):
@@ -168,7 +173,7 @@
             pltpu.VMEM((chips, 2, 8, num_actions + 128), f32),
             pltpu.SemaphoreType.DMA((nblocks,)),
         ],
-        compiler_params=pltpu.CompilerParams(vmem_limit_bytes=40 * 1024 * 1024),
+        compiler_params=pltpu.CompilerParams(vmem_limit_bytes=57 * 1024 * 1024),
         cost_estimate=pl.CostEstimate(flops=3 * 10**9, bytes_accessed=10**7, transcendentals=0),
     )(core, obs0, emb, keys, targets, value_targets, weight, w_pol, w_val, gain, *blocks)
 

time: 202 us -> 196 us (0.970)
  Pallas kernels: 32.5 us -> 28.2 us
  waiting for transfers between devices: 42.1 us -> 37.9 us
    pallas_call x1, Pallas kernels: 32.5 us -> 28.2 us  [run_block(): pl.pallas_call(functools.partial(block_kernel, steps, share, half, nblock...]
    unnamed x22 -> x20, local copies, waits for them, and re-layouts: 3.96 us -> 0.58 us
    all_gather x1, waiting for transfers between devices: 9.09 us -> 6.56 us  [gather_blocks(): lax.all_gather(own, ('table', 'mp'), axis=0, tiled=True, axis_index_group...]
  transfers between devices with their start and end apart: 5 -> 5, of which waited for: 5 -> 5; matrix products, arithmetic and copies ran while one was open for 3% -> 6% of each run, Pallas kernels for 0% -> 0%
where the time goes in v3:
time: 196 us
  blocking collectives  84.7 us (43%)
  waiting for transfers between devices  37.9 us (19%)
  Pallas kernels  28.2 us (14%)
  starting transfers between devices  15.2 us (8%)
  between operations  14.3 us (7%)
  local copies, waits for them, and re-layouts  7.59 us (4%)
  other arithmetic  5.83 us (3%)
  matrix products  2.07 us (1%)
    all_to_all x1, blocking collectives, gather_plane(): lax.all_to_all(jnp.tile(rows, (tables // 2, 1)), 'table', split_axis=0, c...  46.3 us
    all_to_all x1, blocking collectives, reduce_partials(): lax.all_to_all(summed, 'table', split_axis=0, concat_axis=0, tiled=True,...  29.3 us
    pallas_call x1, Pallas kernels, run_block(): pl.pallas_call(functools.partial(block_kernel, steps, share, half, nblock...  28.2 us
    ppermute x1, waiting for transfers between devices, swap_digits(): return lax.ppermute(rows, ('table', 'mp'), swap)  15.1 us
    all_to_all x1, waiting for transfers between devices, deliver_unrolls(): lax.all_to_all(rows, 'table', split_axis=0, concat_axis=0, tiled=True, ax...  13.1 us
    all_to_all x1, blocking collectives, reduce_partials(): lax.all_to_all(copies, 'mp', split_axis=0, concat_axis=0, tiled=True)  9.16 us
    all_gather x1, waiting for transfers between devices, gather_blocks(): lax.all_gather(own, ('table', 'mp'), axis=0, tiled=True, axis_index_group...  6.56 us
    all_to_all x1, starting transfers between devices, deliver_unrolls(): lax.all_to_all(rows, 'table', split_axis=0, concat_axis=0, tiled=True, ax...  6.02 us
  transfers between devices with their start and end apart: 5, of which 5 were waited for; matrix products, arithmetic and copies ran while one was open for 6% of the time, Pallas kernels for 0%

profile of v3, /device:TPU:8, one launch (start us, length us, event | category | flops | bytes accessed | tf_op | source)
XLA Modules:
  0.0 195.9 jit_solution(6004442082110396069)
XLA Ops:
  7.2 0.8 fusion.12
  8.1 1.9 collective-permute-start
  10.0 1.1 collective-permute-done
  11.3 46.3 %all_to_all.24 = bf16[64,16,512]{2,1,0:T(8,128)(2,1)} all-to-all(bf16[64,16,512]{2,1,0:T(8,128)(2,1)S(1)} %tile.4), channel_id=1, replica_groups={{0,8,16,24,32,40,48,56,64,72,80,88,96,104,112,120,128,136,144,152,160,1..., dimensions={0} | all-to-all | bytes 2097152 | tf_op jit(solution)/shard_map/all_to_all | solution.py:206
  58.1 0.7 reduce.20
  58.8 0.7 reduce.19
  60.7 5.1 %collective-permute-start.1 = (bf16[32,8,1024]{2,1,0:T(8,128)(2,1)S(1)}, bf16[32,8,1024]{2,1,0:T(8,128)(2,1)}, u32[]{:S(2)}, u32[]{:S(2)}) collective-permute-start(bf16[32,8,1024]{2,1,0:T(8,128)(2,1)S(1)} %fusion.1), channel_id=1, source_target_pairs={{0,0},{1,4},{2,8},{3,12},{4,1},{5,5},{6,9},{7,13},{8,2},{9,6},{10,... | collective-permute-start | bytes 1572872 | tf_op jit(solution)/shard_map/ppermute | solution.py:250
  65.8 15.1 %collective-permute-done.1 = bf16[32,8,1024]{2,1,0:T(8,128)(2,1)} collective-permute-done((bf16[32,8,1024]{2,1,0:T(8,128)(2,1)S(1)}, bf16[32,8,1024]{2,1,0:T(8,128)(2,1)}, u32[]{:S(2)}, u32[]{:S(2)}) %collective-permute-start.1) | collective-permute-done | bytes 524320 | tf_op jit(solution)/shard_map/ppermute | solution.py:250
  80.9 6.0 %all-to-all-start.1 = ((bf16[32,8,1024]{2,1,0:T(8,128)(2,1)}), bf16[32,8,1024]{2,1,0:T(8,128)(2,1)S(1)}, u32[]{:S(2)}, u32[]{:S(2)}) async-start(bf16[32,8,1024]{2,1,0:T(8,128)(2,1)} %collective-permute-done.1), calls=%async_computation.1 | async-start | bytes 1048576 | tf_op jit(solution)/shard_map/all_to_all | solution.py:256
  88.1 0.7 add.92.keys_ref
  89.0 1.0 convolution_convert_fusion.emb_ref
  90.1 13.1 %all-to-all-done.1 = bf16[32,8,1024]{2,1,0:T(8,128)(2,1)S(1)} async-done(((bf16[32,8,1024]{2,1,0:T(8,128)(2,1)}), bf16[32,8,1024]{2,1,0:T(8,128)(2,1)S(1)}, u32[]{:S(2)}, u32[]{:S(2)}) %all-to-all-start.1) | async-done | bytes 524320 | tf_op jit(solution)/shard_map/all_to_all | solution.py:256
  103.5 0.8 broadcast_in_dim_tile.4.weight_ref
  105.3 0.8 reshape.195.value_targets_ref
  106.6 0.6 slice_bitcast_fusion.obs_ref
  107.3 0.8 fusion.5.targets_ref
  108.1 6.6 %all-gather.2.cloned.1.call-done.rest_0_ = bf16[8192,512]{1,0:T(8,128)(2,1)} async-done(((bf16[1024,512]{1,0:T(8,128)(2,1)}), bf16[8192,512]{1,0:T(8,128)(2,1)}) %all-gather.2.cloned.1.call-update) | async-done | bytes 8388624 | tf_op jit(solution)/shard_map/all_gather | solution.py:221
  114.6 28.2 %shard_map.130 = (f32[64,8,640]{2,1,0:T(8,128)}, bf16[64,8,640]{2,1,0:T(8,128)(2,1)}) custom-call(s32[1]{0:T(128)} %bitcast.core_ref, bf16[32,1024]{1,0:T(8,128)(2,1)} %slice_bitcast_fusion.obs_ref, bf16[160,1024]{1,0:T(8,128)(2,1)} %convolution_convert_fusion.emb_ref, s32[1,640]{1,0:T(1,128)} %add.92.keys_ref, f32[192,256]{1,0:T(8,128)} %fusion.5.targets_ref, ...), custom_call_target="tpu_custom_call" | custom-call | flops 3000000000 | bytes 10000000 | tf_op jit(solution)/shard_map/pallas_call | solution.py:157
  142.8 2.2 %collective-permute-start.2 = (bf16[64,8,640]{2,1,0:T(8,128)(2,1)}, bf16[64,8,640]{2,1,0:T(8,128)(2,1)S(1)}, u32[]{:S(2)}, u32[]{:S(2)}) collective-permute-start(bf16[64,8,640]{2,1,0:T(8,128)(2,1)} %get-tuple-element.8), channel_id=1, source_target_pairs={{0,4},{4,0},{8,12},{12,8},{16,20},{20,16},{24,28},{28,24},{32,36},... | collective-permute-start | bytes 1966088 | tf_op jit(solution)/shard_map/ppermute | solution.py:182
  145.0 2.0 %collective-permute-done.2 = bf16[64,8,640]{2,1,0:T(8,128)(2,1)S(1)} collective-permute-done((bf16[64,8,640]{2,1,0:T(8,128)(2,1)}, bf16[64,8,640]{2,1,0:T(8,128)(2,1)S(1)}, u32[]{:S(2)}, u32[]{:S(2)}) %collective-permute-start.2) | collective-permute-done | bytes 655392 | tf_op jit(solution)/shard_map/ppermute | solution.py:182
  147.0 1.5 add_convert_fusion
  148.5 29.3 %all_to_all.25 = bf16[64,8,640]{2,1,0:T(8,128)(2,1)S(1)} all-to-all(bf16[64,8,640]{2,1,0:T(8,128)(2,1)S(1)} %add_convert_fusion), channel_id=1, replica_groups={{0,8,16,24,32,40,48,56,64,72,80,88,96,104,112,120,128,136,144,152,160,1..., dimensions={0} | all-to-all | bytes 1310720 | tf_op jit(solution)/shard_map/all_to_all | solution.py:264
  178.0 9.2 %all_to_all.26 = f32[4,8,640]{2,1,0:T(8,128)S(1)} all-to-all(f32[4,8,640]{2,1,0:T(8,128)S(1)} %broadcast_in_dim.26), channel_id=1, replica_groups=mesh['table'=128,'mp'=4] {'mp'}, dimensions={0} | all-to-all | bytes 163840 | tf_op jit(solution)/shard_map/all_to_all | solution.py:274
  187.1 0.7 fusion.10
  (60 shorter events, 6.6 us)
Async XLA Ops:
  7.2 53.0 %copy-start = (bf16[512,1024]{1,0:T(8,128)(2,1)S(1)}, bf16[512,1024]{1,0:T(8,128)(2,1)}, u32[]{:S(2)}) copy-start(bf16[512,1024]{1,0:T(8,128)(2,1)} %param.11) | copy-start | bytes 3145732
  7.2 107.4 %all-gather.2.cloned.1.call-start = ((), (), s32[]{:S(2)}) async-start(), calls=%async_computation.4 | async-start | bytes 9437184 | tf_op jit(solution)/shard_map/all_gather | solution.py:221
  8.1 3.1 %collective-permute-start = (bf16[8,512]{1,0:T(8,128)(2,1)S(1)}, bf16[8,512]{1,0:T(8,128)(2,1)S(1)}, u32[]{:S(2)}, u32[]{:S(2)}) collective-permute-start(bf16[8,512]{1,0:T(8,128)(2,1)S(1)} %get-tuple-element.14), channel_id=1, source_target_pairs={{0,4},{4,0},{8,12},{12,8},{16,20},{20,16},{24,28},{28,24},{32,36},... | collective-permute-start | bytes 24584 | tf_op jit(solution)/shard_map/ppermute | solution.py:182
  11.3 46.8 %copy-start.7 = (s32[1,128,1]{1,2,0:T(1,128)S(1)}, s32[1,128,1]{1,2,0:T(1,128)}, u32[]{:S(2)}) copy-start(s32[1,128,1]{1,2,0:T(1,128)} %param.12) | copy-start | bytes 1540
  11.3 47.5 %copy-start.8 = (s32[1,128]{1,0:T(1,128)S(1)}, s32[1,128]{1,0:T(1,128)}, u32[]{:S(2)}) copy-start(s32[1,128]{1,0:T(1,128)} %param.13) | copy-start | bytes 1540
  60.2 26.8 %copy-start.3 = (bf16[1024]{0:T(1024)(128)(2,1)S(1)}, bf16[1024]{0:T(1024)(128)(2,1)}, u32[]{:S(2)}) copy-start(bf16[1024]{0:T(1024)(128)(2,1)} %param.19) | copy-start | bytes 6148
  60.2 27.4 %copy-start.5 = (s32[5,128]{1,0:T(8,128)S(1)}, s32[5,128]{1,0:T(8,128)}, u32[]{:S(2)}) copy-start(s32[5,128]{1,0:T(8,128)} %param.14) | copy-start | bytes 7684
  60.2 28.5 %copy-start.6 = (f32[5,128]{1,0:T(8,128)S(1)}, f32[5,128]{1,0:T(8,128)}, u32[]{:S(2)}) copy-start(f32[5,128]{1,0:T(8,128)} %param.15) | copy-start | bytes 7684
  60.2 28.8 %copy-start.2 = (bf16[256,1024]{1,0:T(8,128)(2,1)S(1)}, bf16[256,1024]{1,0:T(8,128)(2,1)}, u32[]{:S(2)}) copy-start(bf16[256,1024]{1,0:T(8,128)(2,1)} %param.20) | copy-start | bytes 1572868
  60.7 20.2 %collective-permute-start.1 = (bf16[32,8,1024]{2,1,0:T(8,128)(2,1)S(1)}, bf16[32,8,1024]{2,1,0:T(8,128)(2,1)}, u32[]{:S(2)}, u32[]{:S(2)}) collective-permute-start(bf16[32,8,1024]{2,1,0:T(8,128)(2,1)S(1)} %fusion.1), channel_id=1, source_target_pairs={{0,0},{1,4},{2,8},{3,12},{4,1},{5,5},{6,9},{7,13},{8,2},{9,6},{10,... | collective-permute-start | bytes 1572872 | tf_op jit(solution)/shard_map/ppermute | solution.py:250
  80.9 22.2 %all-to-all-start.1 = ((bf16[32,8,1024]{2,1,0:T(8,128)(2,1)}), bf16[32,8,1024]{2,1,0:T(8,128)(2,1)S(1)}, u32[]{:S(2)}, u32[]{:S(2)}) async-start(bf16[32,8,1024]{2,1,0:T(8,128)(2,1)} %collective-permute-done.1), calls=%async_computation.1 | async-start | bytes 1048576 | tf_op jit(solution)/shard_map/all_to_all | solution.py:256
  87.0 17.7 %copy-start.4 = (f32[1024]{0:T(1024)S(1)}, f32[1024]{0:T(1024)}, u32[]{:S(2)}) copy-start(f32[1024]{0:T(1024)} %param.21) | copy-start | bytes 12292
  90.1 16.0 %copy-start.1 = (bf16[1024,256]{1,0:T(8,128)(2,1)S(1)}, bf16[1024,256]{1,0:T(8,128)(2,1)}, u32[]{:S(2)}) copy-start(bf16[1024,256]{1,0:T(8,128)(2,1)} %w_pol_ref.1) | copy-start | bytes 1572868
  142.8 4.2 %collective-permute-start.2 = (bf16[64,8,640]{2,1,0:T(8,128)(2,1)}, bf16[64,8,640]{2,1,0:T(8,128)(2,1)S(1)}, u32[]{:S(2)}, u32[]{:S(2)}) collective-permute-start(bf16[64,8,640]{2,1,0:T(8,128)(2,1)} %get-tuple-element.8), channel_id=1, source_target_pairs={{0,4},{4,0},{8,12},{12,8},{16,20},{20,16},{24,28},{28,24},{32,36},... | collective-permute-start | bytes 1966088 | tf_op jit(solution)/shard_map/ppermute | solution.py:182
Sparse Core Ops, SparseCore 0:
  57.7 56.8 all-gather.1

commit v4 on v3

--- a/solution.py
+++ b/solution.py
@@ -32,22 +32,33 @@
 
 
 def block_kernel(
-    steps, share, half, nblocks, arrays, pieces,
-    core_ref, obs_ref, emb_ref, keys_ref, targets_ref, value_targets_ref, weight_ref, w_pol_ref,
-    w_val_ref, gain_ref, *rest,
+    steps, share, lines, halves,
+    weights_hbm, unorder_hbm, core_ref, start_ref, keys_ref, targets_ref, value_targets_ref, weight_ref, w_pol_ref,
+    w_val_ref, gain_ref, mine_ref, other_ref, weights, unorder, latents, mixeds, slopes, mixed_lows,
+    lows, head_sums, sems,
 ):
-    hbm = rest[:arrays]
-    mine_ref, other_ref = rest[arrays:arrays + 2]
-    weights, latents, mixeds, slopes, lows, head_sums, sems = rest[arrays + 2:]
     chips = mine_ref.shape[0]
     core = core_ref[0]
     width = lows.shape[1]
     parts = lows.shape[0] // (steps * share)
-    copies = []
-    for j, (array, start) in enumerate(pieces):
-        source = hbm[array].at[pl.ds(start, weights.shape[1]), :]
-        copies.append(pltpu.make_async_copy(source, weights.at[j], sems.at[j]))
-        copies[j].start()
+    depth, units = weights.shape[1], weights.shape[2] // 2
+    spans = [slice(side * depth, (side + 1) * depth) for side in range(halves)]
+    copies = [
+        [
+            pltpu.make_async_copy(
+                weights_hbm.at[pl.ds((side * lines + line) * depth, depth), :],
+                weights.at[side * lines + line],
+                sems.at[side * lines + line],
+            )
+            for side in range(halves)
+        ]
+        for line in range(lines)
+    ]
+    for line_copies in copies:
+        for copy in line_copies:
+            copy.start()
+    unorder_copy = pltpu.make_async_copy(unorder_hbm, unorder, sems.at[halves * lines])
+    unorder_copy.start()
     gain = gain_ref[...]
 
     def rows_of(position):
@@ -56,26 +67,36 @@
 
     def forward(position, latent, arriving=False):
         here = rows_of(position)
-        mixed = latent + emb_ref[here, :].astype(f32)
+        mixed = latent + start_ref[here, :].astype(f32)
         mixeds[here, :] = mixed
         normed = (mixed * inverse_scale(mixed) * gain).astype(bf16)
         hiddens = []
-        for j in range(nblocks):
+        for line in range(lines):
             if arriving:
-                copies[j].wait()
-            preact = dot_nn(normed, weights[j, :, :half])
+                for copy in copies[line]:
+                    copy.wait()
+            preact = sum(
+                dot_nn(normed[:, span], weights[side * lines + line, :, :units])
+                for side, span in enumerate(spans)
+            )
             sig = 1.0 / (1.0 + jnp.exp(-preact))
-            slopes[here, j * half:(j + 1) * half] = sig * (1.0 + preact * (1.0 - sig))
+            slopes[here, line * units:(line + 1) * units] = sig * (1.0 + preact * (1.0 - sig))
             hiddens.append((preact * sig).astype(bf16))
-        total = jnp.zeros((mixed.shape[1], share), f32)
-        for j in range(nblocks):
-            total = total + dot_nt(weights[j, :, half:], hiddens[j])
-        total = total.T
+        total = jnp.concatenate(
+            [
+                sum(
+                    dot_nt(weights[side * lines + line, :, units:], hiddens[line])
+                    for line in range(lines)
+                )
+                for side in range(halves)
+            ],
+            axis=0,
+        ).T
         latent = mixed + total
         latents[rows_of(position + 1), :] = latent
         return latent
 
-    first = obs_ref[...].astype(f32)
+    first = start_ref[steps * share:, :].astype(f32)
     latents[:share, :] = first
     lax.fori_loop(1, steps, forward, forward(0, first, arriving=True))
 
@@ -100,8 +121,8 @@
     )
     head_sums[...] = sums.reshape(head_sums.shape)
     columns = sums.shape[1]
-    mine_ref[:, :, :columns] = head_sums[:, core]
-    other_ref[:, :, :columns] = head_sums[:, 1 - core].astype(bf16)
+    mine_ref[:, :, :columns] = head_sums[core].astype(bf16)
+    other_ref[:, :, :columns] = head_sums[1 - core].astype(bf16)
     head_grad = dot_nt(logit_grad, w_pol_ref[...]) + value_grad * w_val
     unit_vec = stacked * scale
     scaled = head_grad * gain
@@ -112,22 +133,33 @@
         here = rows_of(position)
         low = cotangent.astype(bf16)
         preact_grads = []
-        for j in range(nblocks):
-            hidden_grad = dot_nn(low, weights[j, :, half:])
-            preact_grads.append((hidden_grad * slopes[here, j * half:(j + 1) * half]).astype(bf16))
-        total = jnp.zeros((cotangent.shape[1], share), f32)
-        for j in range(nblocks):
-            total = total + dot_nt(weights[j, :, :half], preact_grads[j])
-        total = total.T
+        for line in range(lines):
+            hidden_grad = sum(
+                dot_nn(low[:, span], weights[side * lines + line, :, units:])
+                for side, span in enumerate(spans)
+            )
+            slope = slopes[here, line * units:(line + 1) * units]
+            preact_grads.append((hidden_grad * slope).astype(bf16))
+        total = jnp.concatenate(
+            [
+                sum(
+                    dot_nt(weights[side * lines + line, :, :units], preact_grads[line])
+                    for line in range(lines)
+                )
+                for side in range(halves)
+            ],
+            axis=0,
+        ).T
         mixed_grad = cotangent + norm_back(mixeds[here, :], total, gain)
-        mixed_low = mixed_grad.astype(bf16)
-        for quarter in range(parts):
-            start = pl.multiple_of(quarter * steps * share + position * share, share)
-            lows[pl.ds(start, share), :] = mixed_low[:, quarter * width:(quarter + 1) * width]
+        mixed_lows[here, :] = mixed_grad.astype(bf16)
         return mixed_grad + latents[here, :]
 
     lax.fori_loop(0, steps, backward, latents[steps * share:, :])
 
+    unorder_copy.wait()
+    for quarter in range(parts):
+        quarter_lows = dot_nn(mixed_lows[...], unorder[:, quarter * width:(quarter + 1) * width])
+        lows[quarter * steps * share:(quarter + 1) * steps * share, :] = quarter_lows.astype(bf16)
     row = lax.broadcasted_iota(jnp.int32, (chips * 8, keys_ref.shape[1]), 0)
     row_key = 2 * row - (row & 7)
     for side, target in ((core, mine_ref), (1 - core, other_ref)):
@@ -137,45 +169,46 @@
 
 
 def run_block(
-    core, obs0, emb, actions, targets, value_targets, weight, w_pol, w_val, gain, blocks, chips
+    core, starts, actions, targets, value_targets, weight, w_pol, w_val, gain, blocks, unorder, chips
 ):
-    share, features = obs0.shape
-    steps = emb.shape[0] // share
+    steps, share = actions.shape
+    features = starts.shape[1]
+    halves = 2
+    depth = features // halves
+    units = blocks.shape[1] // 2
+    lines = blocks.shape[0] // features
+    rows = (steps + 1) * share
     num_actions = w_pol.shape[1]
     parts = 8 * chips * 2 // num_actions
     width = features // parts
     columns = num_actions + 128 + width
     quarters = jnp.arange(parts, dtype=jnp.int32)
     keys = (actions.reshape(1, -1) * parts + quarters[:, None]).reshape(1, -1)
-    nblocks = sum(block.shape[0] for block in blocks) // features
-    half = blocks[0].shape[1] // 2
-    rows = (steps + 1) * share
-    pieces = [
-        (i, k * features) for i, block in enumerate(blocks) for k in range(block.shape[0] // features)
-    ]
     vmem = pl.BlockSpec(memory_space=pltpu.VMEM)
     return pl.pallas_call(
-        functools.partial(block_kernel, steps, share, half, nblocks, len(blocks), tuple(pieces)),
+        functools.partial(block_kernel, steps, share, lines, halves),
         out_shape=(
-            jax.ShapeDtypeStruct((chips, 8, columns), f32),
+            jax.ShapeDtypeStruct((chips, 8, columns), bf16),
             jax.ShapeDtypeStruct((chips, 8, columns), bf16),
         ),
-        in_specs=[pl.BlockSpec(memory_space=pltpu.SMEM)]
-        + [vmem] * 9
-        + [pl.BlockSpec(memory_space=pltpu.HBM)] * len(blocks),
+        in_specs=[pl.BlockSpec(memory_space=pltpu.HBM)] * 2
+        + [pl.BlockSpec(memory_space=pltpu.SMEM)]
+        + [vmem] * 8,
         out_specs=(vmem,) * 2,
         scratch_shapes=[
-            pltpu.VMEM((nblocks, features, 2 * half), bf16),
+            pltpu.VMEM((halves * lines, depth, 2 * units), bf16),
+            pltpu.VMEM((features, features), bf16),
             pltpu.VMEM((rows, features), f32),
             pltpu.VMEM((steps * share, features), f32),
-            pltpu.VMEM((steps * share, nblocks * half), f32),
+            pltpu.VMEM((steps * share, lines * units), f32),
+            pltpu.VMEM((steps * share, features), bf16),
             pltpu.VMEM((parts * steps * share, width), bf16),
-            pltpu.VMEM((chips, 2, 8, num_actions + 128), f32),
-            pltpu.SemaphoreType.DMA((nblocks,)),
+            pltpu.VMEM((halves, chips, 8, num_actions + 128), f32),
+            pltpu.SemaphoreType.DMA((halves * lines + 1,)),
         ],
         compiler_params=pltpu.CompilerParams(vmem_limit_bytes=57 * 1024 * 1024),
         cost_estimate=pl.CostEstimate(flops=3 * 10**9, bytes_accessed=10**7, transcendentals=0),
-    )(core, obs0, emb, keys, targets, value_targets, weight, w_pol, w_val, gain, *blocks)
+    )(blocks, unorder, core, starts, keys, targets, value_targets, weight, w_pol, w_val, gain)
 
 
 def cores_swap(value, tables):
@@ -188,18 +221,6 @@
 
 def same_core_groups(tables):
     return [[2 * k + c for k in range(tables // 2)] for c in range(2)]
-
-
-def own_rows_of_weights(w_in, w_out, core, tables):
-    half = w_in.shape[1] // 2
-    low = jnp.concatenate([w_in[:, :half], w_out[:, :half]], axis=1)
-    high = jnp.concatenate([w_in[:, half:], w_out[:, half:]], axis=1)
-    first = core == 0
-    mine = jnp.where(first, low, high)
-    got = cores_swap(jnp.where(first, high, low), tables)
-    return jnp.where(
-        first, jnp.concatenate([mine, got], axis=0), jnp.concatenate([got, mine], axis=0)
-    )
 
 
 def gather_plane(rows, tables):
@@ -218,7 +239,7 @@
         [(2 * k + c) * members + m for c in range(2) for m in range(members)]
         for k in range(tables // 2)
     ]
-    return [lax.all_gather(own, ("table", "mp"), axis=0, tiled=True, axis_index_groups=groups)]
+    return lax.all_gather(own, ("table", "mp"), axis=0, tiled=True, axis_index_groups=groups)
 
 
 def pick_unrolls(replay, request_rows, request_count, steps, member, tables, members):
@@ -260,7 +281,7 @@
 
 def reduce_partials(mine, other, tables, members):
     got = cores_swap(other, tables)
-    summed = (mine + got.astype(f32)).astype(bf16)
+    summed = (mine.astype(f32) + got.astype(f32)).astype(bf16)
     parts = lax.all_to_all(
         summed,
         "table",
@@ -285,9 +306,8 @@
     features = replay.shape[1]
     steps = actions.shape[0]
     num_actions = w_pol.shape[1]
-    own_rows = own_rows_of_weights(w_in, w_out, core, tables)
     rows = pick_unrolls(replay, request_rows, request_count, steps, member, tables, members)
-    own = gather_plane(own_rows, tables)
+    own = gather_plane(jnp.concatenate([w_in, w_out], axis=1), tables)
     blocks = gather_blocks(own, tables, members)
     rows, _ = lax.optimization_barrier((rows, own))
     rows = swap_digits(rows, tables, members)
@@ -313,19 +333,33 @@
     action_ids = jnp.arange(num_actions, dtype=jnp.int32)
     onehots = (actions.reshape(-1)[:, None] == action_ids[None, :]).astype(bf16)
     emb = jnp.dot(onehots, embed, preferred_element_type=f32).astype(bf16)
+    feature_ids = jnp.arange(features, dtype=jnp.int32)
+    order = (feature_ids % (features // 2)) // 8 * 16 + feature_ids // (features // 2) * 8 + feature_ids % 8
+    unorder = (order[:, None] == feature_ids[None, :]).astype(bf16)
+    starts = lax.dot_general(
+        jnp.concatenate([emb, observed[0]], axis=0),
+        unorder,
+        (((1,), (1,)), ((), ())),
+        preferred_element_type=f32,
+    ).astype(bf16)
+
+    def ordered(values):
+        by_rows = values.reshape(features // 16, 2, 8, *values.shape[1:])
+        return jnp.swapaxes(by_rows, 0, 1).reshape(values.shape)
+
     row_weight = jnp.tile(used_rows / tables, steps + 1)
     mine, other = run_block(
         core.reshape(1),
-        observed[0],
-        emb,
+        starts,
         actions,
         policy_targets,
         value_targets.reshape(-1, 1),
         row_weight[:, None],
-        w_pol,
-        w_val[None, :],
-        gain[None, :],
+        ordered(w_pol),
+        ordered(w_val)[None, :],
+        ordered(gain)[None, :],
         blocks,
+        unorder,
         tables // 2,
     )
     rows = reduce_partials(mine, other, tables, members)

time: 196 us -> 192 us (0.980)
  waiting for transfers between devices: 37.9 us -> 32.4 us
  other arithmetic: 5.83 us -> 8.19 us
    ppermute x1, waiting for transfers between devices: 15.1 us -> 12.7 us  [swap_digits(): return lax.ppermute(rows, ('table', 'mp'), swap)]
    ppermute x2 -> x1, starting transfers between devices: 4.11 us -> 2.16 us  [cores_swap(): return lax.ppermute(value, 'table', [(t, t ^ 1) for t in range(tables)])]
  transfers between devices with their start and end apart: 5 -> 4, of which waited for: 5 -> 4; matrix products, arithmetic and copies ran while one was open for 6% -> 8% of each run, Pallas kernels for 0% -> 0%
where the time goes in v4:
time: 192 us
  blocking collectives  83.3 us (43%)
  waiting for transfers between devices  32.4 us (17%)
  Pallas kernels  28.6 us (15%)
  between operations  14.3 us (7%)
  starting transfers between devices  13.6 us (7%)
  other arithmetic  8.19 us (4%)
  local copies, waits for them, and re-layouts  7.98 us (4%)
  matrix products  3.2 us (2%)
    all_to_all x1, blocking collectives, gather_plane(): lax.all_to_all(jnp.tile(rows, (tables // 2, 1)), 'table', split_axis=0, c...  45.7 us
    pallas_call x1, Pallas kernels, run_block(): pl.pallas_call(functools.partial(block_kernel, steps, share, lines, halve...  28.6 us
    all_to_all x1, blocking collectives, reduce_partials(): lax.all_to_all(summed, 'table', split_axis=0, concat_axis=0, tiled=True,...  28.4 us
    ppermute x1, waiting for transfers between devices, swap_digits(): return lax.ppermute(rows, ('table', 'mp'), swap)  12.7 us
    all_to_all x1, waiting for transfers between devices, deliver_unrolls(): lax.all_to_all(rows, 'table', split_axis=0, concat_axis=0, tiled=True, ax...  11.8 us
    all_to_all x1, blocking collectives, reduce_partials(): lax.all_to_all(copies, 'mp', split_axis=0, concat_axis=0, tiled=True)  9.19 us
    all_to_all x1, starting transfers between devices, deliver_unrolls(): lax.all_to_all(rows, 'table', split_axis=0, concat_axis=0, tiled=True, ax...  6.09 us
    all_gather x1, waiting for transfers between devices, gather_blocks(): lax.all_gather(own, ('table', 'mp'), axis=0, tiled=True, axis_index_group...  5.89 us
  transfers between devices with their start and end apart: 4, of which 4 were waited for; matrix products, arithmetic and copies ran while one was open for 8% of the time, Pallas kernels for 0%

profile of v4, /device:TPU:8, one launch (start us, length us, event | category | flops | bytes accessed | tf_op | source)
XLA Modules:
  0.0 191.7 jit_solution(1914818532540740163)
XLA Ops:
  7.2 0.8 pad_maximum_fusion
  8.1 45.7 %all_to_all.24 = bf16[64,8,1024]{2,1,0:T(8,128)(2,1)} all-to-all(bf16[64,8,1024]{2,1,0:T(8,128)(2,1)S(1)} %tile.4), channel_id=1, replica_groups={{0,8,16,24,32,40,48,56,64,72,80,88,96,104,112,120,128,136,144,152,160,1..., dimensions={0} | all-to-all | bytes 2097152 | tf_op jit(solution)/shard_map/all_to_all | solution.py:227
  54.5 0.7 reduce.20
  55.1 0.7 reduce.19
  57.1 5.4 %collective-permute-start = (bf16[32,8,1024]{2,1,0:T(8,128)(2,1)S(1)}, bf16[32,8,1024]{2,1,0:T(8,128)(2,1)}, u32[]{:S(2)}, u32[]{:S(2)}) collective-permute-start(bf16[32,8,1024]{2,1,0:T(8,128)(2,1)S(1)} %fusion.4), channel_id=1, source_target_pairs={{0,0},{1,4},{2,8},{3,12},{4,1},{5,5},{6,9},{7,13},{8,2},{9,6},{10,... | collective-permute-start | bytes 1572872 | tf_op jit(solution)/shard_map/ppermute | solution.py:271
  62.6 0.7 broadcast_in_dim_reshape.8.w_val_ref
  63.4 0.7 broadcast_in_dim_reshape.9.gain_ref
  64.6 12.7 %collective-permute-done = bf16[32,8,1024]{2,1,0:T(8,128)(2,1)} collective-permute-done((bf16[32,8,1024]{2,1,0:T(8,128)(2,1)S(1)}, bf16[32,8,1024]{2,1,0:T(8,128)(2,1)}, u32[]{:S(2)}, u32[]{:S(2)}) %collective-permute-start) | collective-permute-done | bytes 524320 | tf_op jit(solution)/shard_map/ppermute | solution.py:271
  77.3 6.1 %all-to-all-start.1 = ((bf16[32,8,1024]{2,1,0:T(8,128)(2,1)}), bf16[32,8,1024]{2,1,0:T(8,128)(2,1)S(1)}, u32[]{:S(2)}, u32[]{:S(2)}) async-start(bf16[32,8,1024]{2,1,0:T(8,128)(2,1)} %collective-permute-done), calls=%async_computation.1 | async-start | bytes 1048576 | tf_op jit(solution)/shard_map/all_to_all | solution.py:277
  84.2 0.8 copy.47
  85.5 1.8 fusion.1.unorder_hbm
  87.3 11.8 %all-to-all-done.1 = bf16[32,8,1024]{2,1,0:T(8,128)(2,1)S(1)} async-done(((bf16[32,8,1024]{2,1,0:T(8,128)(2,1)}), bf16[32,8,1024]{2,1,0:T(8,128)(2,1)S(1)}, u32[]{:S(2)}, u32[]{:S(2)}) %all-to-all-start.1) | async-done | bytes 524320 | tf_op jit(solution)/shard_map/all_to_all | solution.py:277
  99.4 0.8 broadcast_in_dim_tile.4.weight_ref
  101.2 0.8 reshape.213.value_targets_ref
  102.6 0.8 fusion.12.targets_ref
  103.4 1.9 fusion.5.start_ref
  105.3 5.9 %all-gather.2.cloned.1.call-done.weights_hbm = bf16[4096,1024]{1,0:T(8,128)(2,1)} async-done(((bf16[512,1024]{1,0:T(8,128)(2,1)}), bf16[4096,1024]{1,0:T(8,128)(2,1)}) %all-gather.2.cloned.1.call-update) | async-done | bytes 8388624 | tf_op jit(solution)/shard_map/all_gather | solution.py:242
  111.2 28.6 %shard_map.130 = (bf16[64,8,640]{2,1,0:T(8,128)(2,1)}, bf16[64,8,640]{2,1,0:T(8,128)(2,1)}) custom-call(bf16[4096,1024]{1,0:T(8,128)(2,1)} %all-gather.2.cloned.1.call-done.weights_hbm, bf16[1024,1024]{1,0:T(8,128)(2,1)} %fusion.1.unorder_hbm, s32[1]{0:T(128)} %bitcast.1.core_ref, bf16[192,1024]{1,0:T(8,128)(2,1)} %fusion.5.start_ref, ...), custom_call_target="tpu_custom_call" | custom-call | flops 3000000000 | bytes 10000000 | tf_op jit(solution)/shard_map/pallas_call | solution.py:188
  139.8 2.2 %collective-permute-start.1 = (bf16[64,8,640]{2,1,0:T(8,128)(2,1)}, bf16[64,8,640]{2,1,0:T(8,128)(2,1)S(1)}, u32[]{:S(2)}, u32[]{:S(2)}) collective-permute-start(bf16[64,8,640]{2,1,0:T(8,128)(2,1)} %get-tuple-element.8), channel_id=1, source_target_pairs={{0,4},{4,0},{8,12},{12,8},{16,20},{20,16},{24,28},{28,24},{32,36},... | collective-permute-start | bytes 1966088 | tf_op jit(solution)/shard_map/ppermute | solution.py:215
  141.9 2.0 %collective-permute-done.1 = bf16[64,8,640]{2,1,0:T(8,128)(2,1)S(1)} collective-permute-done((bf16[64,8,640]{2,1,0:T(8,128)(2,1)}, bf16[64,8,640]{2,1,0:T(8,128)(2,1)S(1)}, u32[]{:S(2)}, u32[]{:S(2)}) %collective-permute-start.1) | collective-permute-done | bytes 655392 | tf_op jit(solution)/shard_map/ppermute | solution.py:215
  144.0 1.2 add_convert_fusion
  145.2 28.4 %all_to_all.25 = bf16[64,8,640]{2,1,0:T(8,128)(2,1)S(1)} all-to-all(bf16[64,8,640]{2,1,0:T(8,128)(2,1)S(1)} %add_convert_fusion), channel_id=1, replica_groups={{0,8,16,24,32,40,48,56,64,72,80,88,96,104,112,120,128,136,144,152,160,1..., dimensions={0} | all-to-all | bytes 1310720 | tf_op jit(solution)/shard_map/all_to_all | solution.py:285
  173.7 9.2 %all_to_all.26 = f32[4,8,640]{2,1,0:T(8,128)S(1)} all-to-all(f32[4,8,640]{2,1,0:T(8,128)S(1)} %broadcast_in_dim.20), channel_id=1, replica_groups=mesh['table'=128,'mp'=4] {'mp'}, dimensions={0} | all-to-all | bytes 163840 | tf_op jit(solution)/shard_map/all_to_all | solution.py:295
  183.0 0.7 fusion.36
  (65 shorter events, 7.2 us)
Async XLA Ops:
  7.2 49.4 %copy-start = (bf16[512,1024]{1,0:T(8,128)(2,1)S(1)}, bf16[512,1024]{1,0:T(8,128)(2,1)}, u32[]{:S(2)}) copy-start(bf16[512,1024]{1,0:T(8,128)(2,1)} %param.11) | copy-start | bytes 3145732
  7.2 104.0 %all-gather.2.cloned.1.call-start = ((), (), s32[]{:S(2)}) async-start(), calls=%async_computation.4 | async-start | bytes 9437184 | tf_op jit(solution)/shard_map/all_gather | solution.py:242
  8.0 46.4 %copy-start.7 = (s32[1,128,1]{1,2,0:T(1,128)S(1)}, s32[1,128,1]{1,2,0:T(1,128)}, u32[]{:S(2)}) copy-start(s32[1,128,1]{1,2,0:T(1,128)} %param.12) | copy-start | bytes 1540
  8.0 47.1 %copy-start.8 = (s32[1,128]{1,0:T(1,128)S(1)}, s32[1,128]{1,0:T(1,128)}, u32[]{:S(2)}) copy-start(s32[1,128]{1,0:T(1,128)} %param.13) | copy-start | bytes 1540
  53.9 8.6 %copy-start.4 = (bf16[1024]{0:T(1024)(128)(2,1)S(1)}, bf16[1024]{0:T(1024)(128)(2,1)}, u32[]{:S(2)}) copy-start(bf16[1024]{0:T(1024)(128)(2,1)} %param.19) | copy-start | bytes 6148
  53.9 9.4 %copy-start.3 = (f32[1024]{0:T(1024)S(1)}, f32[1024]{0:T(1024)}, u32[]{:S(2)}) copy-start(f32[1024]{0:T(1024)} %param.21) | copy-start | bytes 12292
  53.9 10.2 %copy-start.5 = (s32[5,128]{1,0:T(8,128)S(1)}, s32[5,128]{1,0:T(8,128)}, u32[]{:S(2)}) copy-start(s32[5,128]{1,0:T(8,128)} %param.14) | copy-start | bytes 7684
  53.9 30.2 %copy-start.6 = (f32[5,128]{1,0:T(8,128)S(1)}, f32[5,128]{1,0:T(8,128)}, u32[]{:S(2)}) copy-start(f32[5,128]{1,0:T(8,128)} %param.15) | copy-start | bytes 7684
  53.9 30.3 %copy-start.1 = (bf16[1024,256]{1,0:T(8,128)(2,1)S(1)}, bf16[1024,256]{1,0:T(8,128)(2,1)}, u32[]{:S(2)}) copy-start(bf16[1024,256]{1,0:T(8,128)(2,1)} %param.18) | copy-start | bytes 1572868
  56.6 28.6 %copy-start.2 = (bf16[256,1024]{1,0:T(8,128)(2,1)S(1)}, bf16[256,1024]{1,0:T(8,128)(2,1)}, u32[]{:S(2)}) copy-start(bf16[256,1024]{1,0:T(8,128)(2,1)} %param.20) | copy-start | bytes 1572868
  57.1 20.2 %collective-permute-start = (bf16[32,8,1024]{2,1,0:T(8,128)(2,1)S(1)}, bf16[32,8,1024]{2,1,0:T(8,128)(2,1)}, u32[]{:S(2)}, u32[]{:S(2)}) collective-permute-start(bf16[32,8,1024]{2,1,0:T(8,128)(2,1)S(1)} %fusion.4), channel_id=1, source_target_pairs={{0,0},{1,4},{2,8},{3,12},{4,1},{5,5},{6,9},{7,13},{8,2},{9,6},{10,... | collective-permute-start | bytes 1572872 | tf_op jit(solution)/shard_map/ppermute | solution.py:271
  77.3 21.8 %all-to-all-start.1 = ((bf16[32,8,1024]{2,1,0:T(8,128)(2,1)}), bf16[32,8,1024]{2,1,0:T(8,128)(2,1)S(1)}, u32[]{:S(2)}, u32[]{:S(2)}) async-start(bf16[32,8,1024]{2,1,0:T(8,128)(2,1)} %collective-permute-done), calls=%async_computation.1 | async-start | bytes 1048576 | tf_op jit(solution)/shard_map/all_to_all | solution.py:277
  139.8 4.2 %collective-permute-start.1 = (bf16[64,8,640]{2,1,0:T(8,128)(2,1)}, bf16[64,8,640]{2,1,0:T(8,128)(2,1)S(1)}, u32[]{:S(2)}, u32[]{:S(2)}) collective-permute-start(bf16[64,8,640]{2,1,0:T(8,128)(2,1)} %get-tuple-element.8), channel_id=1, source_target_pairs={{0,4},{4,0},{8,12},{12,8},{16,20},{20,16},{24,28},{28,24},{32,36},... | collective-permute-start | bytes 1966088 | tf_op jit(solution)/shard_map/ppermute | solution.py:215
Sparse Core Ops, SparseCore 0:
  54.0 57.0 all-gather.1

commit v5 on v4

--- a/solution.py
+++ b/solution.py
@@ -70,7 +70,14 @@
         mixed = latent + start_ref[here, :].astype(f32)
         mixeds[here, :] = mixed
         normed = (mixed * inverse_scale(mixed) * gain).astype(bf16)
+        totals = [0.0] * halves
         hiddens = []
+
+        def add_line(line):
+            for side in range(halves):
+                product = dot_nt(weights[side * lines + line, :, units:], hiddens[line])
+                totals[side] = totals[side] + product
+
         for line in range(lines):
             if arriving:
                 for copy in copies[line]:
@@ -82,16 +89,11 @@
             sig = 1.0 / (1.0 + jnp.exp(-preact))
             slopes[here, line * units:(line + 1) * units] = sig * (1.0 + preact * (1.0 - sig))
             hiddens.append((preact * sig).astype(bf16))
-        total = jnp.concatenate(
-            [
-                sum(
-                    dot_nt(weights[side * lines + line, :, units:], hiddens[line])
-                    for line in range(lines)
-                )
-                for side in range(halves)
-            ],
-            axis=0,
-        ).T
+            if line > 0:
+                add_line(line - 1)
+        for line in range(lines - 1, lines):
+            add_line(line)
+        total = jnp.concatenate(totals, axis=0).T
         latent = mixed + total
         latents[rows_of(position + 1), :] = latent
         return latent
@@ -292,7 +294,39 @@
     )
     summed = jnp.sum(parts.astype(f32), axis=0)
     copies = jnp.broadcast_to(summed[None], (members, *summed.shape))
-    return jnp.sum(lax.all_to_all(copies, "mp", split_axis=0, concat_axis=0, tiled=True), axis=0)
+    return lax.all_to_all(copies, "mp", split_axis=0, concat_axis=0, tiled=True)
+
+
+def unpack_kernel(terms_ref, pol_ref, embed_ref, val_ref):
+    rows = jnp.sum(terms_ref[...], axis=0)
+    num_actions = pol_ref.shape[1]
+    pol_ref[...] = rows[:, :num_actions]
+    value = rows[:, num_actions:num_actions + 1] + rows[:, num_actions + 1:num_actions + 2]
+    val_ref[...] = jnp.broadcast_to(value, (rows.shape[0], 128)).T[:1, :]
+    actions = embed_ref.shape[0]
+    parts = rows.shape[0] // actions
+    start = num_actions + 128
+    width = rows.shape[1] - start
+    for action in range(actions):
+        for part in range(parts):
+            row = action * parts + part
+            embed_ref[action:action + 1, part * width:(part + 1) * width] = rows[row:row + 1, start:]
+
+
+def unpack_gradients(terms, num_actions, actions):
+    rows, columns = terms.shape[1:]
+    parts = rows // actions
+    pol, embed, val = pl.pallas_call(
+        unpack_kernel,
+        out_shape=(
+            jax.ShapeDtypeStruct((rows, num_actions), f32),
+            jax.ShapeDtypeStruct((actions, parts * (columns - num_actions - 128)), f32),
+            jax.ShapeDtypeStruct((1, rows), f32),
+        ),
+        in_specs=[pl.BlockSpec(memory_space=pltpu.VMEM)],
+        out_specs=(pl.BlockSpec(memory_space=pltpu.VMEM),) * 3,
+    )(terms)
+    return pol, embed, val.reshape(rows)
 
 
 def per_device(
@@ -362,11 +396,8 @@
         unorder,
         tables // 2,
     )
-    rows = reduce_partials(mine, other, tables, members)
-    out_pol = rows[:, :num_actions]
-    out_val = rows[:, num_actions] + rows[:, num_actions + 1]
-    out_embed = rows[:, num_actions + 128 :].reshape(num_actions // tables, features)
-    return out_pol, out_embed, out_val
+    terms = reduce_partials(mine, other, tables, members)
+    return unpack_gradients(terms, num_actions, num_actions // tables)
 
 
 def solution(mesh):

time: 192 us -> 191 us (level)
  no operation moved by 1% of the time
where the time goes in v5:
time: 191 us
  blocking collectives  83.4 us (44%)
  waiting for transfers between devices  32.4 us (17%)
  Pallas kernels  29.7 us (16%)
  between operations  14.3 us (7%)
  starting transfers between devices  13.6 us (7%)
  other arithmetic  7.49 us (4%)
  local copies, waits for them, and re-layouts  6.78 us (4%)
  matrix products  3.2 us (2%)
    all_to_all x1, blocking collectives, gather_plane(): lax.all_to_all(jnp.tile(rows, (tables // 2, 1)), 'table', split_axis=0, c...  45.7 us
    all_to_all x1, blocking collectives, reduce_partials(): lax.all_to_all(summed, 'table', split_axis=0, concat_axis=0, tiled=True,...  28.4 us
    pallas_call x1, Pallas kernels, run_block(): pl.pallas_call(functools.partial(block_kernel, steps, share, lines, halve...  28.1 us
    ppermute x1, waiting for transfers between devices, swap_digits(): return lax.ppermute(rows, ('table', 'mp'), swap)  12.7 us
    all_to_all x1, waiting for transfers between devices, deliver_unrolls(): lax.all_to_all(rows, 'table', split_axis=0, concat_axis=0, tiled=True, ax...  11.8 us
    all_to_all x1, blocking collectives, reduce_partials(): return lax.all_to_all(copies, 'mp', split_axis=0, concat_axis=0, tiled=True)  9.26 us
    all_to_all x1, starting transfers between devices, deliver_unrolls(): lax.all_to_all(rows, 'table', split_axis=0, concat_axis=0, tiled=True, ax...  6.09 us
    all_gather x1, waiting for transfers between devices, gather_blocks(): lax.all_gather(own, ('table', 'mp'), axis=0, tiled=True, axis_index_group...  5.89 us
  transfers between devices with their start and end apart: 4, of which 4 were waited for; matrix products, arithmetic and copies ran while one was open for 8% of the time, Pallas kernels for 0%

profile of v5, /device:TPU:8, one launch (start us, length us, event | category | flops | bytes accessed | tf_op | source)
XLA Modules:
  0.0 191.0 jit_solution(1080599158970248117)
XLA Ops:
  7.2 0.8 pad_maximum_fusion
  8.1 45.7 %all_to_all.24 = bf16[64,8,1024]{2,1,0:T(8,128)(2,1)} all-to-all(bf16[64,8,1024]{2,1,0:T(8,128)(2,1)S(1)} %tile.4), channel_id=1, replica_groups={{0,8,16,24,32,40,48,56,64,72,80,88,96,104,112,120,128,136,144,152,160,1..., dimensions={0} | all-to-all | bytes 2097152 | tf_op jit(solution)/shard_map/all_to_all | solution.py:229
  54.5 0.7 reduce.18
  55.1 0.7 reduce.17
  57.1 5.4 %collective-permute-start = (bf16[32,8,1024]{2,1,0:T(8,128)(2,1)S(1)}, bf16[32,8,1024]{2,1,0:T(8,128)(2,1)}, u32[]{:S(2)}, u32[]{:S(2)}) collective-permute-start(bf16[32,8,1024]{2,1,0:T(8,128)(2,1)S(1)} %fusion.4), channel_id=1, source_target_pairs={{0,0},{1,4},{2,8},{3,12},{4,1},{5,5},{6,9},{7,13},{8,2},{9,6},{10,... | collective-permute-start | bytes 1572872 | tf_op jit(solution)/shard_map/ppermute | solution.py:273
  62.6 0.7 broadcast_in_dim_reshape.8.w_val_ref
  63.4 0.7 broadcast_in_dim_reshape.9.gain_ref
  64.6 12.7 %collective-permute-done = bf16[32,8,1024]{2,1,0:T(8,128)(2,1)} collective-permute-done((bf16[32,8,1024]{2,1,0:T(8,128)(2,1)S(1)}, bf16[32,8,1024]{2,1,0:T(8,128)(2,1)}, u32[]{:S(2)}, u32[]{:S(2)}) %collective-permute-start) | collective-permute-done | bytes 524320 | tf_op jit(solution)/shard_map/ppermute | solution.py:273
  77.3 6.1 %all-to-all-start.1 = ((bf16[32,8,1024]{2,1,0:T(8,128)(2,1)}), bf16[32,8,1024]{2,1,0:T(8,128)(2,1)S(1)}, u32[]{:S(2)}, u32[]{:S(2)}) async-start(bf16[32,8,1024]{2,1,0:T(8,128)(2,1)} %collective-permute-done), calls=%async_computation.1 | async-start | bytes 1048576 | tf_op jit(solution)/shard_map/all_to_all | solution.py:279
  84.2 0.8 copy.35
  85.5 1.8 fusion.1.unorder_hbm
  87.3 11.8 %all-to-all-done.1 = bf16[32,8,1024]{2,1,0:T(8,128)(2,1)S(1)} async-done(((bf16[32,8,1024]{2,1,0:T(8,128)(2,1)}), bf16[32,8,1024]{2,1,0:T(8,128)(2,1)S(1)}, u32[]{:S(2)}, u32[]{:S(2)}) %all-to-all-start.1) | async-done | bytes 524320 | tf_op jit(solution)/shard_map/all_to_all | solution.py:279
  99.4 0.8 broadcast_in_dim_tile.4.weight_ref
  101.2 0.8 reshape.212.value_targets_ref
  102.6 0.8 fusion.12.targets_ref
  103.4 1.9 fusion.5.start_ref
  105.3 5.9 %all-gather.2.cloned.1.call-done.weights_hbm = bf16[4096,1024]{1,0:T(8,128)(2,1)} async-done(((bf16[512,1024]{1,0:T(8,128)(2,1)}), bf16[4096,1024]{1,0:T(8,128)(2,1)}) %all-gather.2.cloned.1.call-update) | async-done | bytes 8388624 | tf_op jit(solution)/shard_map/all_gather | solution.py:244
  111.2 28.1 %shard_map.130 = (bf16[64,8,640]{2,1,0:T(8,128)(2,1)}, bf16[64,8,640]{2,1,0:T(8,128)(2,1)}) custom-call(bf16[4096,1024]{1,0:T(8,128)(2,1)} %all-gather.2.cloned.1.call-done.weights_hbm, bf16[1024,1024]{1,0:T(8,128)(2,1)} %fusion.1.unorder_hbm, s32[1]{0:T(128)} %bitcast.1.core_ref, bf16[192,1024]{1,0:T(8,128)(2,1)} %fusion.5.start_ref, ...), custom_call_target="tpu_custom_call" | custom-call | flops 3000000000 | bytes 10000000 | tf_op jit(solution)/shard_map/pallas_call | solution.py:190
  139.2 2.2 %collective-permute-start.1 = (bf16[64,8,640]{2,1,0:T(8,128)(2,1)}, bf16[64,8,640]{2,1,0:T(8,128)(2,1)S(1)}, u32[]{:S(2)}, u32[]{:S(2)}) collective-permute-start(bf16[64,8,640]{2,1,0:T(8,128)(2,1)} %get-tuple-element.11), channel_id=1, source_target_pairs={{0,4},{4,0},{8,12},{12,8},{16,20},{20,16},{24,28},{28,24},{32,36},... | collective-permute-start | bytes 1966088 | tf_op jit(solution)/shard_map/ppermute | solution.py:217
  141.4 2.0 %collective-permute-done.1 = bf16[64,8,640]{2,1,0:T(8,128)(2,1)S(1)} collective-permute-done((bf16[64,8,640]{2,1,0:T(8,128)(2,1)}, bf16[64,8,640]{2,1,0:T(8,128)(2,1)S(1)}, u32[]{:S(2)}, u32[]{:S(2)}) %collective-permute-start.1) | collective-permute-done | bytes 655392 | tf_op jit(solution)/shard_map/ppermute | solution.py:217
  143.4 1.2 add_convert_fusion
  144.7 28.4 %all_to_all.25 = bf16[64,8,640]{2,1,0:T(8,128)(2,1)S(1)} all-to-all(bf16[64,8,640]{2,1,0:T(8,128)(2,1)S(1)} %add_convert_fusion), channel_id=1, replica_groups={{0,8,16,24,32,40,48,56,64,72,80,88,96,104,112,120,128,136,144,152,160,1..., dimensions={0} | all-to-all | bytes 1310720 | tf_op jit(solution)/shard_map/all_to_all | solution.py:287
  173.3 9.3 %all_to_all.26.terms_ref = f32[4,8,640]{2,1,0:T(8,128)} all-to-all(f32[4,8,640]{2,1,0:T(8,128)S(1)} %broadcast_in_dim.20), channel_id=1, replica_groups=mesh['table'=128,'mp'=4] {'mp'}, dimensions={0} | all-to-all | bytes 163840 | tf_op jit(solution)/shard_map/all_to_all | solution.py:297
  182.5 1.6 shard_map.131
  (62 shorter events, 5.9 us)
Async XLA Ops:
  7.2 49.4 %copy-start = (bf16[512,1024]{1,0:T(8,128)(2,1)S(1)}, bf16[512,1024]{1,0:T(8,128)(2,1)}, u32[]{:S(2)}) copy-start(bf16[512,1024]{1,0:T(8,128)(2,1)} %param.11) | copy-start | bytes 3145732
  7.2 104.0 %all-gather.2.cloned.1.call-start = ((), (), s32[]{:S(2)}) async-start(), calls=%async_computation.4 | async-start | bytes 9437184 | tf_op jit(solution)/shard_map/all_gather | solution.py:244
  8.0 46.4 %copy-start.7 = (s32[1,128,1]{1,2,0:T(1,128)S(1)}, s32[1,128,1]{1,2,0:T(1,128)}, u32[]{:S(2)}) copy-start(s32[1,128,1]{1,2,0:T(1,128)} %param.12) | copy-start | bytes 1540
  8.0 47.1 %copy-start.8 = (s32[1,128]{1,0:T(1,128)S(1)}, s32[1,128]{1,0:T(1,128)}, u32[]{:S(2)}) copy-start(s32[1,128]{1,0:T(1,128)} %param.13) | copy-start | bytes 1540
  53.9 8.6 %copy-start.4 = (bf16[1024]{0:T(1024)(128)(2,1)S(1)}, bf16[1024]{0:T(1024)(128)(2,1)}, u32[]{:S(2)}) copy-start(bf16[1024]{0:T(1024)(128)(2,1)} %param.19) | copy-start | bytes 6148
  53.9 9.4 %copy-start.3 = (f32[1024]{0:T(1024)S(1)}, f32[1024]{0:T(1024)}, u32[]{:S(2)}) copy-start(f32[1024]{0:T(1024)} %param.21) | copy-start | bytes 12292
  53.9 10.2 %copy-start.5 = (s32[5,128]{1,0:T(8,128)S(1)}, s32[5,128]{1,0:T(8,128)}, u32[]{:S(2)}) copy-start(s32[5,128]{1,0:T(8,128)} %param.14) | copy-start | bytes 7684
  53.9 30.2 %copy-start.6 = (f32[5,128]{1,0:T(8,128)S(1)}, f32[5,128]{1,0:T(8,128)}, u32[]{:S(2)}) copy-start(f32[5,128]{1,0:T(8,128)} %param.15) | copy-start | bytes 7684
  53.9 30.3 %copy-start.1 = (bf16[1024,256]{1,0:T(8,128)(2,1)S(1)}, bf16[1024,256]{1,0:T(8,128)(2,1)}, u32[]{:S(2)}) copy-start(bf16[1024,256]{1,0:T(8,128)(2,1)} %param.18) | copy-start | bytes 1572868
  56.6 28.6 %copy-start.2 = (bf16[256,1024]{1,0:T(8,128)(2,1)S(1)}, bf16[256,1024]{1,0:T(8,128)(2,1)}, u32[]{:S(2)}) copy-start(bf16[256,1024]{1,0:T(8,128)(2,1)} %param.20) | copy-start | bytes 1572868
  57.1 20.2 %collective-permute-start = (bf16[32,8,1024]{2,1,0:T(8,128)(2,1)S(1)}, bf16[32,8,1024]{2,1,0:T(8,128)(2,1)}, u32[]{:S(2)}, u32[]{:S(2)}) collective-permute-start(bf16[32,8,1024]{2,1,0:T(8,128)(2,1)S(1)} %fusion.4), channel_id=1, source_target_pairs={{0,0},{1,4},{2,8},{3,12},{4,1},{5,5},{6,9},{7,13},{8,2},{9,6},{10,... | collective-permute-start | bytes 1572872 | tf_op jit(solution)/shard_map/ppermute | solution.py:273
  77.3 21.8 %all-to-all-start.1 = ((bf16[32,8,1024]{2,1,0:T(8,128)(2,1)}), bf16[32,8,1024]{2,1,0:T(8,128)(2,1)S(1)}, u32[]{:S(2)}, u32[]{:S(2)}) async-start(bf16[32,8,1024]{2,1,0:T(8,128)(2,1)} %collective-permute-done), calls=%async_computation.1 | async-start | bytes 1048576 | tf_op jit(solution)/shard_map/all_to_all | solution.py:279
  139.2 4.2 %collective-permute-start.1 = (bf16[64,8,640]{2,1,0:T(8,128)(2,1)}, bf16[64,8,640]{2,1,0:T(8,128)(2,1)S(1)}, u32[]{:S(2)}, u32[]{:S(2)}) collective-permute-start(bf16[64,8,640]{2,1,0:T(8,128)(2,1)} %get-tuple-element.11), channel_id=1, source_target_pairs={{0,4},{4,0},{8,12},{12,8},{16,20},{20,16},{24,28},{28,24},{32,36},... | collective-permute-start | bytes 1966088 | tf_op jit(solution)/shard_map/ppermute | solution.py:217
Sparse Core Ops, SparseCore 0:
  54.0 57.0 all-gather.1

commit v6 on v5

--- a/solution.py
+++ b/solution.py
@@ -18,6 +18,11 @@
 
 def dot_nt(a, b):
     return lax.dot_general(a, b, (((1,), (1,)), ((), ())), preferred_element_type=f32)
+
+
+def dot_nt_rows(a, b):
+    rows = a.shape[0] // 2
+    return jnp.concatenate([dot_nt(a[:rows], b), dot_nt(a[rows:], b)], axis=0)
 
 
 def inverse_scale(vector):
@@ -75,7 +80,7 @@
 
         def add_line(line):
             for side in range(halves):
-                product = dot_nt(weights[side * lines + line, :, units:], hiddens[line])
+                product = dot_nt_rows(weights[side * lines + line, :, units:], hiddens[line])
                 totals[side] = totals[side] + product
 
         for line in range(lines):
@@ -145,7 +150,7 @@
         total = jnp.concatenate(
             [
                 sum(
-                    dot_nt(weights[side * lines + line, :, :units], preact_grads[line])
+                    dot_nt_rows(weights[side * lines + line, :, :units], preact_grads[line])
                     for line in range(lines)
                 )
                 for side in range(halves)

time: 191 us -> 191 us (level)
  no operation moved by 1% of the time
where the time goes in v6:
time: 191 us
  blocking collectives  83.4 us (44%)
  waiting for transfers between devices  32.4 us (17%)
  Pallas kernels  29.4 us (15%)
  between operations  14.3 us (7%)
  starting transfers between devices  13.6 us (7%)
  other arithmetic  7.49 us (4%)
  local copies, waits for them, and re-layouts  6.78 us (4%)
  matrix products  3.2 us (2%)
    all_to_all x1, blocking collectives, gather_plane(): lax.all_to_all(jnp.tile(rows, (tables // 2, 1)), 'table', split_axis=0, c...  45.7 us
    all_to_all x1, blocking collectives, reduce_partials(): lax.all_to_all(summed, 'table', split_axis=0, concat_axis=0, tiled=True,...  28.4 us
    pallas_call x1, Pallas kernels, run_block(): pl.pallas_call(functools.partial(block_kernel, steps, share, lines, halve...  27.8 us
    ppermute x1, waiting for transfers between devices, swap_digits(): return lax.ppermute(rows, ('table', 'mp'), swap)  12.7 us
    all_to_all x1, waiting for transfers between devices, deliver_unrolls(): lax.all_to_all(rows, 'table', split_axis=0, concat_axis=0, tiled=True, ax...  11.8 us
    all_to_all x1, blocking collectives, reduce_partials(): return lax.all_to_all(copies, 'mp', split_axis=0, concat_axis=0, tiled=True)  9.27 us
    all_to_all x1, starting transfers between devices, deliver_unrolls(): lax.all_to_all(rows, 'table', split_axis=0, concat_axis=0, tiled=True, ax...  6.09 us
    all_gather x1, waiting for transfers between devices, gather_blocks(): lax.all_gather(own, ('table', 'mp'), axis=0, tiled=True, axis_index_group...  5.89 us
  transfers between devices with their start and end apart: 4, of which 4 were waited for; matrix products, arithmetic and copies ran while one was open for 8% of the time, Pallas kernels for 0%

profile of v6, /device:TPU:8, one launch (start us, length us, event | category | flops | bytes accessed | tf_op | source)
XLA Modules:
  0.0 190.7 jit_solution(3360239839699173435)
XLA Ops:
  7.2 0.8 pad_maximum_fusion
  8.1 45.7 %all_to_all.24 = bf16[64,8,1024]{2,1,0:T(8,128)(2,1)} all-to-all(bf16[64,8,1024]{2,1,0:T(8,128)(2,1)S(1)} %tile.4), channel_id=1, replica_groups={{0,8,16,24,32,40,48,56,64,72,80,88,96,104,112,120,128,136,144,152,160,1..., dimensions={0} | all-to-all | bytes 2097152 | tf_op jit(solution)/shard_map/all_to_all | solution.py:234
  54.5 0.7 reduce.18
  55.1 0.7 reduce.17
  57.1 5.4 %collective-permute-start = (bf16[32,8,1024]{2,1,0:T(8,128)(2,1)S(1)}, bf16[32,8,1024]{2,1,0:T(8,128)(2,1)}, u32[]{:S(2)}, u32[]{:S(2)}) collective-permute-start(bf16[32,8,1024]{2,1,0:T(8,128)(2,1)S(1)} %fusion.4), channel_id=1, source_target_pairs={{0,0},{1,4},{2,8},{3,12},{4,1},{5,5},{6,9},{7,13},{8,2},{9,6},{10,... | collective-permute-start | bytes 1572872 | tf_op jit(solution)/shard_map/ppermute | solution.py:278
  62.6 0.7 broadcast_in_dim_reshape.8.w_val_ref
  63.4 0.7 broadcast_in_dim_reshape.9.gain_ref
  64.6 12.7 %collective-permute-done = bf16[32,8,1024]{2,1,0:T(8,128)(2,1)} collective-permute-done((bf16[32,8,1024]{2,1,0:T(8,128)(2,1)S(1)}, bf16[32,8,1024]{2,1,0:T(8,128)(2,1)}, u32[]{:S(2)}, u32[]{:S(2)}) %collective-permute-start) | collective-permute-done | bytes 524320 | tf_op jit(solution)/shard_map/ppermute | solution.py:278
  77.3 6.1 %all-to-all-start.1 = ((bf16[32,8,1024]{2,1,0:T(8,128)(2,1)}), bf16[32,8,1024]{2,1,0:T(8,128)(2,1)S(1)}, u32[]{:S(2)}, u32[]{:S(2)}) async-start(bf16[32,8,1024]{2,1,0:T(8,128)(2,1)} %collective-permute-done), calls=%async_computation.1 | async-start | bytes 1048576 | tf_op jit(solution)/shard_map/all_to_all | solution.py:284
  84.2 0.8 copy.35
  85.5 1.8 fusion.1.unorder_hbm
  87.3 11.8 %all-to-all-done.1 = bf16[32,8,1024]{2,1,0:T(8,128)(2,1)S(1)} async-done(((bf16[32,8,1024]{2,1,0:T(8,128)(2,1)}), bf16[32,8,1024]{2,1,0:T(8,128)(2,1)S(1)}, u32[]{:S(2)}, u32[]{:S(2)}) %all-to-all-start.1) | async-done | bytes 524320 | tf_op jit(solution)/shard_map/all_to_all | solution.py:284
  99.4 0.8 broadcast_in_dim_tile.4.weight_ref
  101.2 0.8 reshape.212.value_targets_ref
  102.6 0.8 fusion.12.targets_ref
  103.4 1.9 fusion.5.start_ref
  105.3 5.9 %all-gather.2.cloned.1.call-done.weights_hbm = bf16[4096,1024]{1,0:T(8,128)(2,1)} async-done(((bf16[512,1024]{1,0:T(8,128)(2,1)}), bf16[4096,1024]{1,0:T(8,128)(2,1)}) %all-gather.2.cloned.1.call-update) | async-done | bytes 8388624 | tf_op jit(solution)/shard_map/all_gather | solution.py:249
  111.2 27.8 %shard_map.130 = (bf16[64,8,640]{2,1,0:T(8,128)(2,1)}, bf16[64,8,640]{2,1,0:T(8,128)(2,1)}) custom-call(bf16[4096,1024]{1,0:T(8,128)(2,1)} %all-gather.2.cloned.1.call-done.weights_hbm, bf16[1024,1024]{1,0:T(8,128)(2,1)} %fusion.1.unorder_hbm, s32[1]{0:T(128)} %bitcast.1.core_ref, bf16[192,1024]{1,0:T(8,128)(2,1)} %fusion.5.start_ref, ...), custom_call_target="tpu_custom_call" | custom-call | flops 3000000000 | bytes 10000000 | tf_op jit(solution)/shard_map/pallas_call | solution.py:195
  138.9 2.2 %collective-permute-start.1 = (bf16[64,8,640]{2,1,0:T(8,128)(2,1)}, bf16[64,8,640]{2,1,0:T(8,128)(2,1)S(1)}, u32[]{:S(2)}, u32[]{:S(2)}) collective-permute-start(bf16[64,8,640]{2,1,0:T(8,128)(2,1)} %get-tuple-element.11), channel_id=1, source_target_pairs={{0,4},{4,0},{8,12},{12,8},{16,20},{20,16},{24,28},{28,24},{32,36},... | collective-permute-start | bytes 1966088 | tf_op jit(solution)/shard_map/ppermute | solution.py:222
  141.1 2.0 %collective-permute-done.1 = bf16[64,8,640]{2,1,0:T(8,128)(2,1)S(1)} collective-permute-done((bf16[64,8,640]{2,1,0:T(8,128)(2,1)}, bf16[64,8,640]{2,1,0:T(8,128)(2,1)S(1)}, u32[]{:S(2)}, u32[]{:S(2)}) %collective-permute-start.1) | collective-permute-done | bytes 655392 | tf_op jit(solution)/shard_map/ppermute | solution.py:222
  143.1 1.2 add_convert_fusion
  144.4 28.4 %all_to_all.25 = bf16[64,8,640]{2,1,0:T(8,128)(2,1)S(1)} all-to-all(bf16[64,8,640]{2,1,0:T(8,128)(2,1)S(1)} %add_convert_fusion), channel_id=1, replica_groups={{0,8,16,24,32,40,48,56,64,72,80,88,96,104,112,120,128,136,144,152,160,1..., dimensions={0} | all-to-all | bytes 1310720 | tf_op jit(solution)/shard_map/all_to_all | solution.py:292
  173.0 9.3 %all_to_all.26.terms_ref = f32[4,8,640]{2,1,0:T(8,128)} all-to-all(f32[4,8,640]{2,1,0:T(8,128)S(1)} %broadcast_in_dim.20), channel_id=1, replica_groups=mesh['table'=128,'mp'=4] {'mp'}, dimensions={0} | all-to-all | bytes 163840 | tf_op jit(solution)/shard_map/all_to_all | solution.py:302
  182.2 1.6 shard_map.131
  (62 shorter events, 5.9 us)
Async XLA Ops:
  7.2 49.4 %copy-start = (bf16[512,1024]{1,0:T(8,128)(2,1)S(1)}, bf16[512,1024]{1,0:T(8,128)(2,1)}, u32[]{:S(2)}) copy-start(bf16[512,1024]{1,0:T(8,128)(2,1)} %param.11) | copy-start | bytes 3145732
  7.2 104.0 %all-gather.2.cloned.1.call-start = ((), (), s32[]{:S(2)}) async-start(), calls=%async_computation.4 | async-start | bytes 9437184 | tf_op jit(solution)/shard_map/all_gather | solution.py:249
  8.0 46.4 %copy-start.7 = (s32[1,128,1]{1,2,0:T(1,128)S(1)}, s32[1,128,1]{1,2,0:T(1,128)}, u32[]{:S(2)}) copy-start(s32[1,128,1]{1,2,0:T(1,128)} %param.12) | copy-start | bytes 1540
  8.0 47.1 %copy-start.8 = (s32[1,128]{1,0:T(1,128)S(1)}, s32[1,128]{1,0:T(1,128)}, u32[]{:S(2)}) copy-start(s32[1,128]{1,0:T(1,128)} %param.13) | copy-start | bytes 1540
  53.9 8.6 %copy-start.4 = (bf16[1024]{0:T(1024)(128)(2,1)S(1)}, bf16[1024]{0:T(1024)(128)(2,1)}, u32[]{:S(2)}) copy-start(bf16[1024]{0:T(1024)(128)(2,1)} %param.19) | copy-start | bytes 6148
  53.9 9.4 %copy-start.3 = (f32[1024]{0:T(1024)S(1)}, f32[1024]{0:T(1024)}, u32[]{:S(2)}) copy-start(f32[1024]{0:T(1024)} %param.21) | copy-start | bytes 12292
  53.9 10.2 %copy-start.5 = (s32[5,128]{1,0:T(8,128)S(1)}, s32[5,128]{1,0:T(8,128)}, u32[]{:S(2)}) copy-start(s32[5,128]{1,0:T(8,128)} %param.14) | copy-start | bytes 7684
  53.9 30.2 %copy-start.6 = (f32[5,128]{1,0:T(8,128)S(1)}, f32[5,128]{1,0:T(8,128)}, u32[]{:S(2)}) copy-start(f32[5,128]{1,0:T(8,128)} %param.15) | copy-start | bytes 7684
  53.9 30.3 %copy-start.1 = (bf16[1024,256]{1,0:T(8,128)(2,1)S(1)}, bf16[1024,256]{1,0:T(8,128)(2,1)}, u32[]{:S(2)}) copy-start(bf16[1024,256]{1,0:T(8,128)(2,1)} %param.18) | copy-start | bytes 1572868
  56.6 28.6 %copy-start.2 = (bf16[256,1024]{1,0:T(8,128)(2,1)S(1)}, bf16[256,1024]{1,0:T(8,128)(2,1)}, u32[]{:S(2)}) copy-start(bf16[256,1024]{1,0:T(8,128)(2,1)} %param.20) | copy-start | bytes 1572868
  57.1 20.2 %collective-permute-start = (bf16[32,8,1024]{2,1,0:T(8,128)(2,1)S(1)}, bf16[32,8,1024]{2,1,0:T(8,128)(2,1)}, u32[]{:S(2)}, u32[]{:S(2)}) collective-permute-start(bf16[32,8,1024]{2,1,0:T(8,128)(2,1)S(1)} %fusion.4), channel_id=1, source_target_pairs={{0,0},{1,4},{2,8},{3,12},{4,1},{5,5},{6,9},{7,13},{8,2},{9,6},{10,... | collective-permute-start | bytes 1572872 | tf_op jit(solution)/shard_map/ppermute | solution.py:278
  77.3 21.8 %all-to-all-start.1 = ((bf16[32,8,1024]{2,1,0:T(8,128)(2,1)}), bf16[32,8,1024]{2,1,0:T(8,128)(2,1)S(1)}, u32[]{:S(2)}, u32[]{:S(2)}) async-start(bf16[32,8,1024]{2,1,0:T(8,128)(2,1)} %collective-permute-done), calls=%async_computation.1 | async-start | bytes 1048576 | tf_op jit(solution)/shard_map/all_to_all | solution.py:284
  138.9 4.2 %collective-permute-start.1 = (bf16[64,8,640]{2,1,0:T(8,128)(2,1)}, bf16[64,8,640]{2,1,0:T(8,128)(2,1)S(1)}, u32[]{:S(2)}, u32[]{:S(2)}) collective-permute-start(bf16[64,8,640]{2,1,0:T(8,128)(2,1)} %get-tuple-element.11), channel_id=1, source_target_pairs={{0,4},{4,0},{8,12},{12,8},{16,20},{20,16},{24,28},{28,24},{32,36},... | collective-permute-start | bytes 1966088 | tf_op jit(solution)/shard_map/ppermute | solution.py:222
Sparse Core Ops, SparseCore 0:
  54.0 57.0 all-gather.1
